TPU v7x, 32 devices: a whole 2x2x4 slice. The times are simulated.
32 devices in a mesh: seq: 8 (over z, x), head: 4 (over y, core).
Axes of the slice: x: 2, y: 2, z: 4, core: 2. Of those that a mesh axis runs over, the one named last changes fastest.
Arguments:
- tokens: bfloat16 [16384, 2048], P('seq'), may hold values from -6 to 6
- norm_gain: float32 [2048], replicated, may hold values from 0.5 to 2
- in_weight: bfloat16 [2048, 3, 2048], P(None, None, 'head')
- out_weight: bfloat16 [2048, 2048], P('head'), may hold values from -0.125 to 0.125
- pattern: int32 [128, 4], replicated, may hold values from 0 to 127, as said below
Outputs:
- mixed: bfloat16 [16384, 2048], P(('seq', 'head'))
Inputs may be any that keep to these rules, and one draw needn't show every extreme that they name: `pattern`: row i names first tile i itself, then 4 - 1 distinct tiles held by other indices of seq (index = tile // 16). Among the rows of one index of seq, at most 10 of these later entries name tiles of any one other index, and every index has one such other index that it names exactly 10 times.
All inputs are finite; a program needn't handle non-finite values.
Results may differ from a plain program's by a relative error of at most 0.019.
Values may be sent and summed in bfloat16 or wider, within the bound.
A program may use at most 128 MiB of HBM per device.

v0:
```python
import math

import jax
import jax.numpy as jnp
from jax import lax
from jax.sharding import PartitionSpec as P

HD = 128
TILE = 128
KT = 4


def normalize(tokens, norm_gain):
    values = tokens.astype(jnp.float32)
    mean_square = jnp.mean(values * values, axis=-1, keepdims=True)
    return (values * lax.rsqrt(mean_square + 1e-05) * norm_gain).astype(jnp.bfloat16)


def by_request(keyvals, pattern, my_rows, shards, myself, tile_count):
    entries = tile_count * (KT - 1)
    capacity = max(2, 3 * entries // (2 * (shards - 1)))
    wanted = pattern.reshape(shards, tile_count, KT)[:, :, 1:].reshape(shards, entries)
    owners = wanted // tile_count
    local_tile = wanted % tile_count
    owned_here = owners == myself
    ranking = jnp.cumsum(owned_here.astype(jnp.int32), axis=1) - 1
    slot_ids = jnp.arange(capacity, dtype=jnp.int32)
    select = owned_here[:, None, :] & (ranking[:, None, :] == slot_ids[None, :, None])
    filled = jnp.any(select, axis=2)
    chosen = jnp.sum(jnp.where(select, local_tile[:, None, :], 0), axis=2)
    outgoing = jnp.where(filled[:, :, None, None], keyvals[chosen], jnp.zeros((), keyvals.dtype))
    incoming = lax.all_to_all(outgoing, "seq", split_axis=0, concat_axis=0, tiled=True)
    sources = my_rows[:, 1:].reshape(entries) // tile_count
    one_hot = (sources[:, None] == jnp.arange(shards, dtype=jnp.int32)[None, :]).astype(jnp.int32)
    running = jnp.cumsum(one_hot, axis=0)
    position = jnp.sum(running * one_hot, axis=1) - 1
    flat_index = sources * capacity + position
    fetched = incoming.reshape(shards * capacity, TILE, keyvals.shape[2])[flat_index]
    return fetched.reshape(tile_count, KT - 1, TILE, keyvals.shape[2])


def body(tokens, norm_gain, in_weight, out_weight, pattern):
    shards = lax.axis_size("seq")
    myself = lax.axis_index("seq")
    row_count = tokens.shape[0]
    tile_count = row_count // TILE
    head_width = in_weight.shape[2]
    head_count = head_width // HD
    normed = normalize(tokens, norm_gain)
    projected = jnp.dot(
        normed,
        in_weight.reshape(in_weight.shape[0], 3 * head_width),
        preferred_element_type=jnp.float32,
    ).astype(jnp.bfloat16)
    projected = projected.reshape(row_count, 3, head_width)
    queries = projected[:, 0].reshape(tile_count, TILE, head_count, HD)
    keyvals = jnp.concatenate([projected[:, 1], projected[:, 2]], axis=1).reshape(
        tile_count, TILE, 2 * head_width
    )
    my_rows = lax.dynamic_slice_in_dim(pattern, myself * tile_count, tile_count, 0)
    fetched = by_request(keyvals, pattern, my_rows, shards, myself, tile_count)
    gathered = jnp.concatenate([keyvals[:, None], fetched], axis=1).reshape(
        tile_count, KT * TILE, 2 * head_width
    )
    key_block = gathered[:, :, :head_width].reshape(tile_count, KT * TILE, head_count, HD)
    value_block = gathered[:, :, head_width:].reshape(tile_count, KT * TILE, head_count, HD)
    scores = jnp.einsum(
        "tqhd,tkhd->thqk", queries, key_block, preferred_element_type=jnp.float32
    ) * (1.0 / math.sqrt(HD))
    maxima = jnp.max(scores, axis=-1, keepdims=True)
    exponent = jnp.exp(scores - maxima)
    weights = (exponent / jnp.sum(exponent, axis=-1, keepdims=True)).astype(jnp.bfloat16)
    attended = jnp.einsum(
        "thqk,tkhd->tqhd", weights, value_block, preferred_element_type=jnp.float32
    ).astype(jnp.bfloat16)
    attended = attended.reshape(row_count, head_width)
    return lax.psum_scatter(
        jnp.dot(attended, out_weight, preferred_element_type=jnp.float32).astype(jnp.bfloat16),
        "head",
        scatter_dimension=0,
        tiled=True,
    )


def solution(mesh):
    return jax.shard_map(
        body,
        mesh=mesh,
        in_specs=(P("seq", None), P(), P(None, None, "head"), P("head", None), P()),
        out_specs=P(("seq", "head"), None),
        check_vma=False,
    )
```

profile of v0, /device:TPU:0, one launch (start us, length us, event | category | flops | bytes accessed | tf_op | source)
XLA Modules:
  0.0 738.7 jit_solution(7204451391019460849)
XLA Ops:
  6.5 9.0 %copy.27 = bf16[2048,3,512]{0,2,1:T(8,128)(2,1)} copy(bf16[2048,3,512]{2,0,1:T(8,128)(2,1)} %param.7) | data formatting | bytes 12582912 | tf_op args[2]
  15.5 5.2 fusion.1
  20.8 0.5 copy-done.1
  21.3 16.1 %fusion.13 = bf16[2048,1536]{0,1:T(8,128)(2,1)S(1)} fusion(bf16[2048,1536]{0,1:T(8,128)(2,1)} %bitcast.57, bf16[2048,2048]{1,0:T(8,128)(2,1)S(1)} %copy-done.1, f32[2048]{0:T(1024)S(1)} %copy-done.3, f32[2048]{0:T(1024)S(1)} %add_rsqrt_fusion), kind=kOutput, calls=%fused_computation.19 | convolution fusion | flops 12904824832 | bytes 20987904 | tf_op jit(solution)/shard_map/dot_general | solution.py:50
  37.4 2.8 slice_bitcast_fusion
  40.2 3.9 copy.29
  44.2 3.9 copy.28
  49.4 4.8 pad_maximum_fusion.1
  54.2 10.9 %gather_fusion = bf16[80,128,1024]{2,1,0:T(8,128)(2,1)} fusion(bf16[16,128,1024]{2,1,0:T(8,128)(2,1)} %pad_maximum_fusion.1, s32[1024]{0:T(1024)S(1)} %pad_clamp_fusion.1), kind=kCustom, calls=%fused_computation | custom fusion | bytes 41943360 | tf_op jit(solution)/shard_map/gather | solution.py:31
  65.1 17.4 %broadcast_select_fusion = bf16[8,10,128,1024]{3,2,1,0:T(8,128)(2,1)} fusion(bf16[8,10,128,1024]{3,2,1,0:T(8,128)(2,1)} %bitcast.46, pred[8,10]{1,0:T(8,128)(4,1)S(1)} %copy.35), kind=kLoop, calls=%fused_computation.5 | loop fusion | flops 10485760 | bytes 41943120 | tf_op jit(solution)/shard_map/jit(_where)/select_n | solution.py:31
  82.6 7.4 all-to-all-start
  90.7 3.5 copy.50
  94.4 449.0 %all-to-all-done = bf16[8,10,128,1024]{3,2,1,0:T(8,128)(2,1)} async-done(((bf16[8,10,128,1024]{3,2,1,0:T(8,128)(2,1)}), bf16[8,10,128,1024]{3,2,1,0:T(8,128)(2,1)}, u32[]{:S(2)}, u32[]{:S(2)}) %all-to-all-start) | async-done | bytes 20971552 | tf_op jit(solution)/shard_map/all_to_all | solution.py:32
  543.4 13.2 %gather_fusion.1 = bf16[48,128,1024]{2,1,0:T(8,128)(2,1)} fusion(bf16[80,128,1024]{2,1,0:T(8,128)(2,1)} %bitcast.8, s32[1024]{0:T(1024)S(1)} %pad_clamp_fusion), kind=kCustom, calls=%fused_computation.1 | custom fusion | bytes 25166016 | tf_op jit(solution)/shard_map/gather | solution.py:38
  556.6 7.9 %pad_maximum_fusion = bf16[16,4,128,1024]{3,2,1,0:T(8,128)(2,1)S(1)} fusion(bf16[16,3,128,1024]{3,2,1,0:T(8,128)(2,1)} %bitcast.49, bf16[16,1,128,512]{3,2,1,0:T(8,128)(2,1)} %bitcast.51, bf16[16,1,128,512]{3,2,1,0:T(8,128)(2,1)} %bitcast.53), kind=kLoop, calls=%fused_computation.9 | loop fusion | flops 50331648 | bytes 33554432 | tf_op jit(solution)/shard_map/concatenate | solution.py:62
  564.6 6.3 fusion.37
  570.8 12.3 %copy.48 = bf16[16,512,512]{1,2,0:T(8,128)(2,1)} copy(bf16[16,512,512]{2,1,0:T(8,128)(2,1)} %get-tuple-element.8) | data formatting | bytes 16777216
  583.1 12.3 %copy.49 = bf16[16,512,512]{1,2,0:T(8,128)(2,1)} copy(bf16[16,512,512]{2,1,0:T(8,128)(2,1)} %get-tuple-element.7) | data formatting | bytes 16777216
  595.4 12.1 %fusion.18 = f32[16,4,128,512]{3,2,1,0:T(8,128)} fusion(bf16[16,512,4,128]{1,3,2,0:T(8,128)(2,1)} %bitcast.48, bf16[16,128,4,128]{1,0,3,2:T(8,128)(2,1)} %bitcast.54), kind=kOutput, calls=%fused_computation.25 | convolution fusion | flops 1073741824 | bytes 27262976 | tf_op jit(solution)/shard_map/tqhd,tkhd->thqk/dot_general | solution.py:67
  607.6 14.7 %fusion.38 = f32[16,4,128]{2,1,0:T(4,128)S(1)} fusion(f32[16,4,128,512]{3,2,1,0:T(8,128)} %fusion.18), kind=kOutput, calls=%fused_computation.66 | output fusion | flops 16777728 | bytes 16809984 | tf_op jit(solution)/shard_map/sub | solution.py:71
  622.2 28.9 %convert_bitcast_fusion = bf16[16,128,4,128]{1,3,2,0:T(8,128)(2,1)} fusion(bf16[16,512,4,128]{1,3,2,0:T(8,128)(2,1)} %bitcast.55, f32[16,4,128]{2,1,0:T(4,128)S(1)} %fusion.38, f32[16,4,128,512]{3,2,1,0:T(8,128)} %fusion.18), kind=kOutput, calls=%fused_computation.27 | convolution fusion | flops 1095770624 | bytes 27295744 | tf_op jit(solution)/shard_map/thqk,tkhd->tqhd/dot_general | solution.py:73
  651.1 2.9 copy.45
  654.0 7.1 convolution_convert_fusion
  661.2 70.7 %reduce-scatter.2.cloned.1.call-done = bf16[512,2048]{1,0:T(8,128)(2,1)} async-done(((bf16[2048,2048]{1,0:T(8,128)(2,1)}), bf16[512,2048]{1,0:T(8,128)(2,1)}) %reduce-scatter.2.cloned.1.call-update) | async-done | bytes 2097168 | tf_op jit(solution)/shard_map/reduce_scatter | solution.py:77
  (36 shorter events, 2.2 us)
Async XLA Ops:
  6.5 647.5 %copy-start = (bf16[512,2048]{1,0:T(8,128)(2,1)S(1)}, bf16[512,2048]{1,0:T(8,128)(2,1)}, u32[]{:S(2)}) copy-start(bf16[512,2048]{1,0:T(8,128)(2,1)} %param.8) | copy-start | bytes 6291460
  6.5 14.2 %copy-start.3 = (f32[2048]{0:T(1024)S(1)}, f32[2048]{0:T(1024)}, u32[]{:S(2)}) copy-start(f32[2048]{0:T(1024)} %param.6) | copy-start | bytes 24580
  15.5 5.8 copy-start.1
  37.4 10.7 %copy-start.2 = (s32[128,4]{0,1:T(4,128)S(1)}, s32[128,4]{0,1:T(4,128)}, u32[]{:S(2)}) copy-start(s32[128,4]{0,1:T(4,128)} %param.9) | copy-start | bytes 6148
  82.6 460.8 %all-to-all-start = ((bf16[8,10,128,1024]{3,2,1,0:T(8,128)(2,1)}), bf16[8,10,128,1024]{3,2,1,0:T(8,128)(2,1)}, u32[]{:S(2)}, u32[]{:S(2)}) async-start(bf16[8,10,128,1024]{3,2,1,0:T(8,128)(2,1)} %broadcast_select_fusion), calls=%async_computation | async-start | bytes 41943040 | tf_op jit(solution)/shard_map/all_to_all | solution.py:32
  90.0 641.9 %reduce-scatter.2.cloned.1.call-start = ((), (), s32[]{:S(2)}) async-start(), calls=%async_computation.2 | async-start | bytes 10485760 | tf_op jit(solution)/shard_map/reduce_scatter | solution.py:77
Sparse Core Ops, SparseCore 0:
  661.3 70.5 reduce-scatter.1
where the time goes:
time: 740 us; the launch traced here: 739 us
  waiting for transfers between devices  520 us (70%)
  local copies, waits for them, and re-layouts  82.5 us (11%)
  matrix products  64.2 us (9%)
  other arithmetic  51.2 us (7%)
  between operations  13.5 us (2%)
  starting transfers between devices  7.6 us (1%)
    all_to_all x1, waiting for transfers between devices, by_request(): lax.all_to_all(outgoing, 'seq', split_axis=0, concat_axis=0, tiled=True)  449 us
    reduce_scatter x1, waiting for transfers between devices, body(): lax.psum_scatter(jnp.dot(attended, out_weight, preferred_element_type=jnp...  70.7 us
    unnamed x14, local copies, waits for them, and re-layouts  40.5 us
    dot_general x1, matrix products, body(): jnp.einsum('thqk,tkhd->tqhd', weights, value_block, preferred_element_typ...  28.9 us
    select_n x1, other arithmetic, by_request(): jnp.where(filled[:, :, None, None], keyvals[chosen], jnp.zeros((), keyval...  17.4 us
    dot_general x1, matrix products, body(): jnp.dot(normed, in_weight.reshape(in_weight.shape[0], 3 * head_width), pr...  16.1 us
  transfers between devices with their start and end apart: 2, of which 2 were waited for; matrix products, arithmetic and copies ran while one was open for 1% of the time, Pallas kernels for 0%

commit v1 on v0

--- a/solution.py
+++ b/solution.py
@@ -3,11 +3,20 @@
 import jax
 import jax.numpy as jnp
 from jax import lax
+from jax.experimental import pallas as pl
+from jax.experimental.pallas import tpu as pltpu
+from jax.sharding import Mesh
 from jax.sharding import PartitionSpec as P
 
 HD = 128
 TILE = 128
 KT = 4
+ZS, XS, YS, CS = 4, 2, 2, 2
+PARTS = YS * CS
+ORDER = ((0, 1, 2, 3), (1, 0, 2, 3), (2, 3, 1, 0), (3, 2, 1, 0))
+SWAP = ((0, 1), (1, 0))
+OWN_SLOTS = 20
+VMEM = 48 * 1024 * 1024
 
 
 def normalize(tokens, norm_gain):
@@ -82,7 +91,212 @@
     )
 
 
+def project_kernel(count, *refs):
+    blocks, weight, out = refs[:count], refs[count], refs[-1]
+    rows = jnp.concatenate([ref[...] for ref in blocks], axis=1)
+    tiles, height, depth = rows.shape
+    product = jnp.dot(
+        rows.reshape(tiles * height, depth), weight[...], preferred_element_type=jnp.float32
+    )
+    out[...] = product.astype(out.dtype).reshape(tiles, height, out.shape[2])
+
+
+def project(pieces, weight, slots, base, step, buffer):
+    tiles, depth = pieces[0].shape[0], pieces[0].shape[2]
+    width = weight.shape[1]
+    in_specs = [pl.BlockSpec((step, p.shape[1], depth), lambda i: (i, 0, 0)) for p in pieces]
+    in_specs.append(pl.BlockSpec((depth, width), lambda i: (0, 0)))
+    operands = list(pieces) + [weight]
+    aliases = {}
+    if buffer is not None:
+        aliases = {len(operands): 0}
+        in_specs.append(pl.BlockSpec(memory_space=pl.ANY))
+        operands.append(buffer)
+    rows = tiles * TILE
+    return pl.pallas_call(
+        lambda *refs: project_kernel(len(pieces), *refs),
+        grid=(tiles // step,),
+        in_specs=in_specs,
+        out_specs=pl.BlockSpec((step, TILE, width), lambda i: (base // step + i, 0, 0)),
+        out_shape=jax.ShapeDtypeStruct((slots, TILE, width), jnp.bfloat16),
+        input_output_aliases=aliases,
+        compiler_params=pltpu.CompilerParams(vmem_limit_bytes=VMEM),
+        cost_estimate=pl.CostEstimate(
+            flops=2 * rows * depth * width,
+            bytes_accessed=2 * (rows * depth + depth * width + rows * width),
+            transcendentals=0,
+        ),
+    )(*operands)
+
+
+def attend_kernel(tile_ids, slot_ids, query, *refs):
+    blocks, out = refs[:KT], refs[KT]
+    width = query.shape[1]
+    for head in range(width // HD):
+        at = slice(head * HD, (head + 1) * HD)
+        at_value = slice(width + head * HD, width + (head + 1) * HD)
+        keys = jnp.concatenate([ref[0, :, at] for ref in blocks], axis=0)
+        values = jnp.concatenate([ref[0, :, at_value] for ref in blocks], axis=0)
+        scores = lax.dot_general(
+            query[:, at], keys, (((1,), (1,)), ((), ())), preferred_element_type=jnp.float32
+        ) * (1.0 / math.sqrt(HD))
+        exponent = jnp.exp(scores - jnp.max(scores, axis=-1, keepdims=True))
+        total = jnp.sum(exponent, axis=-1, keepdims=True)
+        summed = jnp.dot(
+            exponent.astype(jnp.bfloat16), values, preferred_element_type=jnp.float32
+        )
+        out[:, at] = (summed / total).astype(out.dtype)
+
+
+def attend(tile_ids, slot_ids, queries, buffer):
+    tiles, width = tile_ids.shape[0], queries.shape[1]
+
+    def at_slot(k):
+        return lambda i, tile_ids, slot_ids: (slot_ids[i * KT + k], 0, 0)
+
+    return pl.pallas_call(
+        attend_kernel,
+        grid_spec=pltpu.PrefetchScalarGridSpec(
+            num_scalar_prefetch=2,
+            grid=(tiles,),
+            in_specs=[pl.BlockSpec((TILE, width), lambda i, tile_ids, slot_ids: (tile_ids[i], 0))]
+            + [pl.BlockSpec((1, TILE, 2 * width), at_slot(k)) for k in range(KT)],
+            out_specs=pl.BlockSpec((TILE, width), lambda i, tile_ids, slot_ids: (i, 0)),
+        ),
+        out_shape=jax.ShapeDtypeStruct((tiles * TILE, width), jnp.bfloat16),
+        compiler_params=pltpu.CompilerParams(vmem_limit_bytes=VMEM),
+        cost_estimate=pl.CostEstimate(
+            flops=4 * tiles * TILE * KT * TILE * width,
+            bytes_accessed=2 * tiles * TILE * width * (2 + 2 * KT),
+            transcendentals=tiles * TILE * KT * TILE * (width // HD),
+        ),
+    )(tile_ids, slot_ids, queries, *([buffer] * KT))
+
+
+def request_lists(rows, shards, tile_count, capacity):
+    entries = rows.reshape(-1)
+    owned = (entries // tile_count)[None, :] == jnp.arange(shards, dtype=jnp.int32)[:, None]
+    rank = jnp.cumsum(owned.astype(jnp.int32), axis=1) - 1
+    slot_ids = jnp.arange(capacity, dtype=jnp.int32)
+    select = owned[:, None, :] & (rank[:, None, :] == slot_ids[None, :, None])
+    chosen = jnp.sum(jnp.where(select, (entries % tile_count)[None, None, :], 0), axis=2)
+    return chosen, jnp.sum(jnp.where(owned, rank, 0), axis=0)
+
+
+def grid_body(tokens, norm_gain, in_weight, out_weight, pattern):
+    shards = ZS * XS
+    z, x = lax.axis_index("z"), lax.axis_index("x")
+    y, c = lax.axis_index("y"), lax.axis_index("c")
+    me, beside = z * XS + x, z * XS + (1 - x)
+    rows, depth = tokens.shape
+    tile_count = rows // TILE
+    entries = tile_count * (KT - 1)
+    capacity = max(2, 3 * entries // (2 * (shards - 1)))
+    head_width = in_weight.shape[2]
+    share = TILE // PARTS
+    order = jnp.asarray(ORDER, jnp.int32)[z]
+
+    tiles = tokens.reshape(tile_count, PARTS, share, depth)
+    mine = lax.dynamic_index_in_dim(tiles, y * CS + c, 1, keepdims=False)
+    block = normalize(mine, norm_gain)
+
+    ups, downs = [block], [block]
+    for s in range(1, ZS):
+        ups.append(lax.ppermute(ups[-1], "z", [(i, i + 1) for i in range(s - 1, ZS - 1)]))
+        downs.append(lax.ppermute(downs[-1], "z", [(i, i - 1) for i in range(1, ZS - s + 1)]))
+
+    my_rows = lax.dynamic_slice_in_dim(pattern, me * tile_count, tile_count, 0)[:, 1:]
+    beside_rows = lax.dynamic_slice_in_dim(pattern, beside * tile_count, tile_count, 0)[:, 1:]
+    my_lists, my_rank = request_lists(my_rows, shards, tile_count, capacity)
+    beside_lists, _ = request_lists(beside_rows, shards, tile_count, capacity)
+
+    def column_block(k):
+        parts = []
+        for at in range(ZS):
+            source = ORDER[at][k]
+            parts.append(ups[at - source] if source <= at else downs[source - at])
+        out = parts[0]
+        for at in range(1, ZS):
+            if parts[at] is not parts[at - 1]:
+                out = jnp.where(z >= at, parts[at], out)
+        return out
+
+    pieces = []
+    for k in range(ZS):
+        held = block if k == 0 else column_block(k)
+        source = order[k] * XS + x
+        out = held[beside_lists[source]]
+        came = lax.ppermute(out, "x", SWAP)
+        if k:
+            pieces.append(held[my_lists[source]])
+        pieces.append(came)
+
+    normed = normalize(tokens, norm_gain)
+    queries = jnp.dot(
+        normed, in_weight[:, 0, :], preferred_element_type=jnp.float32
+    ).astype(jnp.bfloat16)
+    weight = in_weight[:, 1:, :].reshape(depth, 2 * head_width)
+    slots = OWN_SLOTS + capacity * len(pieces)
+    buffer = project([normed.reshape(tile_count, TILE, depth)], weight, slots, 0, 4, None)
+    for at, piece in enumerate(pieces):
+        across = lax.ppermute(piece, "y", SWAP)
+        sides = lax.ppermute(piece, "c", SWAP)
+        corner = lax.ppermute(across, "c", SWAP)
+        buffer = project(
+            [piece, across, sides, corner], weight, slots,
+            OWN_SLOTS + at * capacity, capacity // 2, buffer,
+        )
+
+    w_across = lax.ppermute(out_weight, "y", SWAP)
+    w_sides = lax.ppermute(out_weight, "c", SWAP)
+    w_corner = lax.ppermute(w_across, "c", SWAP)
+    out_all = jnp.concatenate([out_weight, w_across, w_sides, w_corner], axis=0)
+
+    owner = my_rows // tile_count
+    step_of = jnp.sum(
+        jnp.where(
+            order[None, None, :] == (owner // XS)[:, :, None],
+            jnp.arange(ZS, dtype=jnp.int32)[None, None, :],
+            0,
+        ),
+        axis=2,
+    )
+    place = 2 * step_of - jnp.where(owner % XS == x, 1, 0)
+    far_slots = OWN_SLOTS + place * capacity + my_rank.reshape(tile_count, KT - 1)
+    slot_ids = jnp.concatenate(
+        [jnp.arange(tile_count, dtype=jnp.int32)[:, None], far_slots], axis=1
+    )
+
+    half = tile_count // YS
+    near = jnp.arange(half, dtype=jnp.int32)
+
+    def attend_half(which):
+        ids = which * half + near
+        picked = lax.dynamic_slice_in_dim(slot_ids, which * half, half, 0)
+        return attend(ids, picked.reshape(-1), queries, buffer)
+
+    far = attend_half(1 - y)
+    far_came = lax.ppermute(far, "y", SWAP)
+    own = attend_half(y)
+    quarter = own.shape[0] // CS
+    keep = [lax.dynamic_slice_in_dim(a, c * quarter, quarter, 0) for a in (own, far_came)]
+    give = [lax.dynamic_slice_in_dim(a, (1 - c) * quarter, quarter, 0) for a in (own, far_came)]
+    came = [lax.ppermute(a, "c", SWAP) for a in give]
+    attended = jnp.concatenate(keep + came, axis=1)
+    return jnp.dot(attended, out_all, preferred_element_type=jnp.float32).astype(jnp.bfloat16)
+
+
 def solution(mesh):
+    if mesh.devices.shape == (ZS * XS, YS * CS):
+        grid = Mesh(mesh.devices.reshape(ZS, XS, YS, CS), ("z", "x", "y", "c"))
+        seq, head = ("z", "x"), ("y", "c")
+        return jax.shard_map(
+            grid_body,
+            mesh=grid,
+            in_specs=(P(seq, None), P(), P(None, None, head), P(head, None), P()),
+            out_specs=P(seq + head, None),
+            check_vma=False,
+        )
     return jax.shard_map(
         body,
         mesh=mesh,

time: 740 us -> 466 us (0.63)
  waiting for transfers between devices: 520 us -> 250 us
  Pallas kernels: 0 us -> 105 us
  local copies, waits for them, and re-layouts: 82.5 us -> 33.7 us
  matrix products: 64.2 us -> 16.3 us
  other arithmetic: 51.2 us -> 25.6 us
  starting transfers between devices: 7.6 us -> 32.4 us
  between operations: 13.5 us -> 2.93 us
    all_to_all x1 -> x0, waiting for transfers between devices: 449 us -> none  [by_request(): lax.all_to_all(outgoing, 'seq', split_axis=0, concat_axis=0, tiled=True)]
    ppermute x0 -> x37, waiting for transfers between devices: none -> 250 us  [the longest x7 125 us: grid_body(): across = lax.ppermute(piece, 'y', SWAP)]
    pallas_call x0 -> x10, Pallas kernels: none -> 105 us  [the longest x8 80.9 us: project(): pl.pallas_call(lambda *refs: project_kernel(len(pieces), *refs), grid=(ti...]
    reduce_scatter x1 -> x0, waiting for transfers between devices: 70.7 us -> none  [body(): lax.psum_scatter(jnp.dot(attended, out_weight, preferred_element_type=jnp...]
    dot_general x4 -> x2, matrix products: 64.2 us -> 16.3 us  [the longest x1 8.49 us: grid_body(): jnp.dot(normed, in_weight[:, 0, :], preferred_element_type=jnp.float32)]
    ppermute x0 -> x37, starting transfers between devices: none -> 32.4 us  [the longest x3 9.07 us: grid_body(): lax.ppermute(ups[-1], 'z', [(i, i + 1) for i in range(s - 1, ZS - 1)])]
    unnamed x14 -> x17, local copies, waits for them, and re-layouts: 40.5 us -> 8.99 us
    sub x1 -> x2, other arithmetic: 14.7 us -> 0.03 us  [request_lists(): rank = jnp.cumsum(owned.astype(jnp.int32), axis=1) - 1]
  transfers between devices with their start and end apart: 2 -> 37, of which waited for: 2 -> 15; matrix products, arithmetic and copies ran while one was open for 1% -> 13% of each run, Pallas kernels for 0% -> 23%
where the time goes in v1:
time: 466 us; the launch traced here: 465 us
  waiting for transfers between devices  250 us (54%)
  Pallas kernels  105 us (23%)
  local copies, waits for them, and re-layouts  33.7 us (7%)
  starting transfers between devices  32.4 us (7%)
  other arithmetic  25.6 us (5%)
  matrix products  16.3 us (3%)
    ppermute x7, waiting for transfers between devices, grid_body(): across = lax.ppermute(piece, 'y', SWAP)  125 us
    pallas_call x8, Pallas kernels, project(): pl.pallas_call(lambda *refs: project_kernel(len(pieces), *refs), grid=(ti...  80.9 us
    ppermute x3, waiting for transfers between devices, grid_body(): lax.ppermute(downs[-1], 'z', [(i, i - 1) for i in range(1, ZS - s + 1)])  62.3 us
    ppermute x3, waiting for transfers between devices, grid_body(): lax.ppermute(ups[-1], 'z', [(i, i + 1) for i in range(s - 1, ZS - 1)])  38 us
    pallas_call x2, Pallas kernels, attend(): pl.pallas_call(attend_kernel, grid_spec=pltpu.PrefetchScalarGridSpec(num_...  23.9 us
    ppermute x1, waiting for transfers between devices, grid_body(): far_came = lax.ppermute(far, 'y', SWAP)  11.5 us
    convert_element_type x2, other arithmetic, normalize(): (values * lax.rsqrt(mean_square + 1e-05) * norm_gain).astype(jnp.bfloat16)  10.8 us
    ppermute x4, waiting for transfers between devices, grid_body(): came = lax.ppermute(out, 'x', SWAP)  10.8 us
  transfers between devices with their start and end apart: 37, of which 15 were waited for; matrix products, arithmetic and copies ran while one was open for 13% of the time, Pallas kernels for 23%

profile of v1, /device:TPU:0, one launch (start us, length us, event | category | flops | bytes accessed | tf_op | source)
XLA Modules:
  0.0 465.4 jit_solution(15781690238174228944)
XLA Ops:
  4.3 6.3 %collective-permute-start = (bf16[16,32,2048]{2,1,0:T(8,128)(2,1)S(1)}, bf16[16,32,2048]{2,1,0:T(8,128)(2,1)}, u32[]{:S(2)}, u32[]{:S(2)}) collective-permute-start(bf16[16,32,2048]{2,1,0:T(8,128)(2,1)S(1)} %fusion.13), channel_id=1, source_target_pairs={{0,8},{8,16},{16,24},{1,9},{9,17},{17,25},{2,10},{10,18},{18,26},{... | collective-permute-start | bytes 6291464 | tf_op jit(solution)/shard_map/ppermute | solution.py:205
  16.1 38.0 %collective-permute-done = bf16[16,32,2048]{2,1,0:T(8,128)(2,1)} collective-permute-done((bf16[16,32,2048]{2,1,0:T(8,128)(2,1)S(1)}, bf16[16,32,2048]{2,1,0:T(8,128)(2,1)}, u32[]{:S(2)}, u32[]{:S(2)}) %collective-permute-start) | collective-permute-done | bytes 2097184 | tf_op jit(solution)/shard_map/ppermute | solution.py:205
  65.4 42.8 %collective-permute-done.4 = bf16[16,32,2048]{2,1,0:T(8,128)(2,1)} collective-permute-done((bf16[16,32,2048]{2,1,0:T(8,128)(2,1)}, bf16[16,32,2048]{2,1,0:T(8,128)(2,1)}, u32[]{:S(2)}, u32[]{:S(2)}) %collective-permute-start.4) | collective-permute-done | bytes 2097184 | tf_op jit(solution)/shard_map/ppermute | solution.py:206
  116.3 22.2 %collective-permute-done.28.refs_1_ = bf16[10,32,2048]{2,1,0:T(8,128)(2,1)} collective-permute-done((bf16[10,32,2048]{2,1,0:T(8,128)(2,1)}, bf16[10,32,2048]{2,1,0:T(8,128)(2,1)}, u32[]{:S(2)}, u32[]{:S(2)}) %collective-permute-start.28) | collective-permute-done | bytes 1310752 | tf_op jit(solution)/shard_map/ppermute | solution.py:242
  139.8 16.0 %collective-permute-done.5 = bf16[16,32,2048]{2,1,0:T(8,128)(2,1)} collective-permute-done((bf16[16,32,2048]{2,1,0:T(8,128)(2,1)}, bf16[16,32,2048]{2,1,0:T(8,128)(2,1)}, u32[]{:S(2)}, u32[]{:S(2)}) %collective-permute-start.5) | collective-permute-done | bytes 2097184 | tf_op jit(solution)/shard_map/ppermute | solution.py:206
  155.8 6.5 %fusion.14 = (bf16[16,32,2048]{2,1,0:T(8,128)(2,1)S(1)}, bf16[16,32,2048]{2,1,0:T(8,128)(2,1)}, bf16[16,32,2048]{2,1,0:T(8,128)(2,1)}) fusion(bf16[16,32,2048]{2,1,0:T(8,128)(2,1)} %collective-permute-done, bf16[16,32,2048]{2,1,0:T(8,128)(2,1)} %collective-permute-done.3, pred[]{:T(512)S(6)} %ge.8, pred[]{:T(512)S(6)} %ge.7, pred[]{:T(512)S(6)} %ge.6, ...), kind=kLoop, calls=%fused_computation.27 | loop fusion | flops 9437184 | bytes 18874372 | tf_op jit(solution)/shard_map/jit(_where)/select_n | solution.py:221
  168.8 8.6 %fusion.2 = bf16[2048,2048]{1,0:T(8,128)(2,1)} fusion(bf16[2048,2048]{1,0:T(8,128)(2,1)} %param.6, f32[2048]{0:T(1024)S(1)} %copy-done.6, f32[2048]{0:T(1024)S(1)} %add_rsqrt_fusion.1), kind=kLoop, calls=%fused_computation.11 | loop fusion | flops 16777216 | bytes 16793600 | tf_op jit(solution)/shard_map/convert_element_type | solution.py:25
  212.4 12.0 %shard_map.64.refs_5_ = bf16[90,128,1024]{2,1,0:T(8,128)(2,1)} custom-call(bf16[16,128,2048]{2,1,0:T(8,128)(2,1)} %bitcast.57, bf16[2048,1024]{1,0:T(8,128)(2,1)S(1)} %bitcast.54), custom_call_target="tpu_custom_call" | custom-call | flops 8589934592 | bytes 16777216 | tf_op jit(solution)/shard_map/pallas_call | solution.py:116
  227.3 21.6 %collective-permute-done.10.refs_1_ = bf16[10,32,2048]{2,1,0:T(8,128)(2,1)} collective-permute-done((bf16[10,32,2048]{2,1,0:T(8,128)(2,1)S(1)}, bf16[10,32,2048]{2,1,0:T(8,128)(2,1)}, u32[]{:S(2)}, u32[]{:S(2)}) %collective-permute-start.10) | collective-permute-done | bytes 1310752 | tf_op jit(solution)/shard_map/ppermute | solution.py:242
  255.5 8.5 %convolution_convert_fusion.query = bf16[2048,512]{1,0:T(8,128)(2,1)S(1)} fusion(bf16[2048,2048]{1,0:T(8,128)(2,1)} %fusion.2, bf16[2048,3,512]{2,0,1:T(8,128)(2,1)} %param.8), kind=kOutput, calls=%fused_computation.29 | convolution fusion | flops 4296015872 | bytes 12582912 | tf_op jit(solution)/shard_map/dot_general | solution.py:235
  265.1 11.9 %collective-permute-done.21.refs_1_ = bf16[10,32,2048]{2,1,0:T(8,128)(2,1)} collective-permute-done((bf16[10,32,2048]{2,1,0:T(8,128)(2,1)}, bf16[10,32,2048]{2,1,0:T(8,128)(2,1)}, u32[]{:S(2)}, u32[]{:S(2)}) %collective-permute-start.21) | collective-permute-done | bytes 1310752 | tf_op jit(solution)/shard_map/ppermute | solution.py:242
  279.4 25.7 %collective-permute-done.14.refs_1_ = bf16[10,32,2048]{2,1,0:T(8,128)(2,1)} collective-permute-done((bf16[10,32,2048]{2,1,0:T(8,128)(2,1)}, bf16[10,32,2048]{2,1,0:T(8,128)(2,1)}, u32[]{:S(2)}, u32[]{:S(2)}) %collective-permute-start.14) | collective-permute-done | bytes 1310752 | tf_op jit(solution)/shard_map/ppermute | solution.py:242
  305.1 10.3 %shard_map.65.refs_5_ = bf16[90,128,1024]{2,1,0:T(8,128)(2,1)} custom-call(bf16[10,32,2048]{2,1,0:T(8,128)(2,1)} %collective-permute-done.27.refs_0_, bf16[10,32,2048]{2,1,0:T(8,128)(2,1)} %collective-permute-done.28.refs_1_, bf16[10,32,2048]{2,1,0:T(8,128)(2,1)} %collective-permute-done.29.refs_2_, ...), custom_call_target="tpu_custom_call", output_to_operand_aliasing={{}: (5, {})} | custom-call | flops 5368709120 | bytes 12058624 | tf_op jit(solution)/shard_map/pallas_call | solution.py:116
  315.4 9.9 %shard_map.66.refs_5_ = bf16[90,128,1024]{2,1,0:T(8,128)(2,1)} custom-call(bf16[10,32,2048]{2,1,0:T(8,128)(2,1)} %gather_fusion.5, bf16[10,32,2048]{2,1,0:T(8,128)(2,1)} %collective-permute-done.24.refs_1_, bf16[10,32,2048]{2,1,0:T(8,128)(2,1)} %collective-permute-done.25.refs_2_, ...), custom_call_target="tpu_custom_call", output_to_operand_aliasing={{}: (5, {})} | custom-call | flops 5368709120 | bytes 12058624 | tf_op jit(solution)/shard_map/pallas_call | solution.py:116
  325.8 10.1 %shard_map.67.refs_5_ = bf16[90,128,1024]{2,1,0:T(8,128)(2,1)} custom-call(bf16[10,32,2048]{2,1,0:T(8,128)(2,1)} %collective-permute-done.20.refs_0_, bf16[10,32,2048]{2,1,0:T(8,128)(2,1)} %collective-permute-done.21.refs_1_, bf16[10,32,2048]{2,1,0:T(8,128)(2,1)} %collective-permute-done.22.refs_2_, ...), custom_call_target="tpu_custom_call", output_to_operand_aliasing={{}: (5, {})} | custom-call | flops 5368709120 | bytes 12058624 | tf_op jit(solution)/shard_map/pallas_call | solution.py:116
  335.9 41.4 %collective-permute-done.7.refs_1_ = bf16[10,32,2048]{2,1,0:T(8,128)(2,1)S(1)} collective-permute-done((bf16[10,32,2048]{2,1,0:T(8,128)(2,1)}, bf16[10,32,2048]{2,1,0:T(8,128)(2,1)S(1)}, u32[]{:S(2)}, u32[]{:S(2)}) %collective-permute-start.7) | collective-permute-done | bytes 1310752 | tf_op jit(solution)/shard_map/ppermute | solution.py:242
  377.8 9.9 %shard_map.68.refs_5_ = bf16[90,128,1024]{2,1,0:T(8,128)(2,1)} custom-call(bf16[10,32,2048]{2,1,0:T(8,128)(2,1)S(1)} %copy-done.2, bf16[10,32,2048]{2,1,0:T(8,128)(2,1)} %collective-permute-done.17.refs_1_, bf16[10,32,2048]{2,1,0:T(8,128)(2,1)} %collective-permute-done.18.refs_2_, ...), custom_call_target="tpu_custom_call", output_to_operand_aliasing={{}: (5, {})} | custom-call | flops 5368709120 | bytes 12058624 | tf_op jit(solution)/shard_map/pallas_call | solution.py:116
  387.7 9.9 %shard_map.69.refs_5_ = bf16[90,128,1024]{2,1,0:T(8,128)(2,1)} custom-call(bf16[10,32,2048]{2,1,0:T(8,128)(2,1)} %collective-permute-done.13.refs_0_, bf16[10,32,2048]{2,1,0:T(8,128)(2,1)} %collective-permute-done.14.refs_1_, bf16[10,32,2048]{2,1,0:T(8,128)(2,1)} %collective-permute-done.15.refs_2_, ...), custom_call_target="tpu_custom_call", output_to_operand_aliasing={{}: (5, {})} | custom-call | flops 5368709120 | bytes 12058624 | tf_op jit(solution)/shard_map/pallas_call | solution.py:116
  398.1 9.3 %shard_map.70.refs_5_ = bf16[90,128,1024]{2,1,0:T(8,128)(2,1)} custom-call(bf16[10,32,2048]{2,1,0:T(8,128)(2,1)S(1)} %gather_fusion.1, bf16[10,32,2048]{2,1,0:T(8,128)(2,1)} %collective-permute-done.10.refs_1_, bf16[10,32,2048]{2,1,0:T(8,128)(2,1)S(1)} %collective-permute-done.11.refs_2_, ...), custom_call_target="tpu_custom_call", output_to_operand_aliasing={{}: (5, {})} | custom-call | flops 5368709120 | bytes 12058624 | tf_op jit(solution)/shard_map/pallas_call | solution.py:116
  407.4 9.7 %shard_map.71.refs_0_.refs_1_.refs_2_.refs_3_ = bf16[90,128,1024]{2,1,0:T(8,128)(2,1)} custom-call(bf16[10,32,2048]{2,1,0:T(8,128)(2,1)} %collective-permute-done.6.refs_0_, bf16[10,32,2048]{2,1,0:T(8,128)(2,1)S(1)} %collective-permute-done.7.refs_1_, bf16[10,32,2048]{2,1,0:T(8,128)(2,1)S(1)} %collective-permute-done.8.refs_2_, ...), custom_call_target="tpu_custom_call", output_to_operand_aliasing={{}: (5, {})} | custom-call | flops 5368709120 | bytes 12058624 | tf_op jit(solution)/shard_map/pallas_call | solution.py:116
  417.1 12.0 %shard_map.73 = bf16[1024,512]{1,0:T(8,128)(2,1)S(1)} custom-call(s32[8]{0:T(128)S(1)} %iota_add_fusion.tile_ids, s32[32]{0:T(128)S(1)} %reshape.420.slot_ids, bf16[2048,512]{1,0:T(8,128)(2,1)S(1)} %convolution_convert_fusion.query, bf16[90,128,1024]{2,1,0:T(8,128)(2,1)} %shard_map.71.refs_0_.refs_1_.refs_2_.refs_3_, ...), custom_call_target="tpu_custom_call" | custom-call | flops 1073741824 | bytes 10485760 | tf_op jit(solution)/shard_map/pallas_call | solution.py:157
  430.7 12.0 %shard_map.72 = bf16[1024,512]{1,0:T(8,128)(2,1)S(1)} custom-call(s32[8]{0:T(128)S(1)} %iota_add_fusion.1.tile_ids, s32[32]{0:T(128)S(1)} %reshape.415.slot_ids, bf16[2048,512]{1,0:T(8,128)(2,1)S(1)} %convolution_convert_fusion.query, bf16[90,128,1024]{2,1,0:T(8,128)(2,1)} %shard_map.71.refs_0_.refs_1_.refs_2_.refs_3_, ...), custom_call_target="tpu_custom_call" | custom-call | flops 1073741824 | bytes 10485760 | tf_op jit(solution)/shard_map/pallas_call | solution.py:157
  442.9 11.5 %collective-permute-done.31 = bf16[1024,512]{1,0:T(8,128)(2,1)} collective-permute-done((bf16[1024,512]{1,0:T(8,128)(2,1)S(1)}, bf16[1024,512]{1,0:T(8,128)(2,1)}, u32[]{:S(2)}, u32[]{:S(2)}) %collective-permute-start.31) | collective-permute-done | bytes 1048608 | tf_op jit(solution)/shard_map/ppermute | solution.py:279
  457.6 7.8 %fusion.15 = bf16[512,2048]{1,0:T(8,128)(2,1)} fusion(bf16[512,2048]{1,0:T(8,128)(2,1)} %collective-permute-done.36, bf16[512,2048]{1,0:T(8,128)(2,1)} %collective-permute-done.35, bf16[512,2048]{1,0:T(8,128)(2,1)} %collective-permute-done.34, bf16[512,2048]{1,0:T(8,128)(2,1)} %param.9, bf16[512,512]{1,0:T(8,128)(2,1)S(1)} %collective-permute-done.33, ...), kind=kOutput, calls=%fused_computation.28 | convolution fusion | flops 4337958912 | bytes 12582912 | tf_op jit(solution)/shard_map/dot_general | solution.py:286
  (143 shorter events, 88.9 us)
Async XLA Ops:
  4.3 49.8 %collective-permute-start = (bf16[16,32,2048]{2,1,0:T(8,128)(2,1)S(1)}, bf16[16,32,2048]{2,1,0:T(8,128)(2,1)}, u32[]{:S(2)}, u32[]{:S(2)}) collective-permute-start(bf16[16,32,2048]{2,1,0:T(8,128)(2,1)S(1)} %fusion.13), channel_id=1, source_target_pairs={{0,8},{8,16},{16,24},{1,9},{9,17},{17,25},{2,10},{10,18},{18,26},{... | collective-permute-start | bytes 6291464 | tf_op jit(solution)/shard_map/ppermute | solution.py:205
  10.5 49.1 %collective-permute-start.3 = (bf16[16,32,2048]{2,1,0:T(8,128)(2,1)S(1)}, bf16[16,32,2048]{2,1,0:T(8,128)(2,1)}, u32[]{:S(2)}, u32[]{:S(2)}) collective-permute-start(bf16[16,32,2048]{2,1,0:T(8,128)(2,1)S(1)} %fusion.13), channel_id=1, source_target_pairs={{8,0},{16,8},{24,16},{9,1},{17,9},{25,17},{10,2},{18,10},{26,18},{... | collective-permute-start | bytes 6291464 | tf_op jit(solution)/shard_map/ppermute | solution.py:206
  59.6 48.5 %collective-permute-start.4 = (bf16[16,32,2048]{2,1,0:T(8,128)(2,1)}, bf16[16,32,2048]{2,1,0:T(8,128)(2,1)}, u32[]{:S(2)}, u32[]{:S(2)}) collective-permute-start(bf16[16,32,2048]{2,1,0:T(8,128)(2,1)} %collective-permute-done.3), channel_id=1, source_target_pairs={{8,0},{16,8},{9,1},{17,9},{10,2},{18,10},{11,3},{19,11},{12,4},{20... | collective-permute-start | bytes 6291464 | tf_op jit(solution)/shard_map/ppermute | solution.py:206
  62.3 47.2 %collective-permute-start.27 = (bf16[10,32,2048]{2,1,0:T(8,128)(2,1)S(1)}, bf16[10,32,2048]{2,1,0:T(8,128)(2,1)}, u32[]{:S(2)}, u32[]{:S(2)}) collective-permute-start(bf16[10,32,2048]{2,1,0:T(8,128)(2,1)S(1)} %gather_fusion.6), channel_id=1, source_target_pairs={{0,4},{4,0},{1,5},{5,1},{2,6},{6,2},{3,7},{7,3},{8,12},{12,8},{9,1... | collective-permute-start | bytes 3932168 | tf_op jit(solution)/shard_map/ppermute | solution.py:229
  64.6 73.9 %collective-permute-start.2 = (bf16[16,32,2048]{2,1,0:T(8,128)(2,1)}, bf16[16,32,2048]{2,1,0:T(8,128)(2,1)S(1)}, u32[]{:S(2)}, u32[]{:S(2)}) collective-permute-start(bf16[16,32,2048]{2,1,0:T(8,128)(2,1)} %collective-permute-done.1), channel_id=1, source_target_pairs={{16,24},{17,25},{18,26},{19,27},{20,28},{21,29},{22,30},{23,31}} | collective-permute-start | bytes 6291464 | tf_op jit(solution)/shard_map/ppermute | solution.py:205
  108.2 47.6 %collective-permute-start.5 = (bf16[16,32,2048]{2,1,0:T(8,128)(2,1)}, bf16[16,32,2048]{2,1,0:T(8,128)(2,1)}, u32[]{:S(2)}, u32[]{:S(2)}) collective-permute-start(bf16[16,32,2048]{2,1,0:T(8,128)(2,1)} %collective-permute-done.4), channel_id=1, source_target_pairs={{8,0},{9,1},{10,2},{11,3},{12,4},{13,5},{14,6},{15,7}} | collective-permute-start | bytes 6291464 | tf_op jit(solution)/shard_map/ppermute | solution.py:206
  116.3 72.9 %collective-permute-start.29 = (bf16[10,32,2048]{2,1,0:T(8,128)(2,1)}, bf16[10,32,2048]{2,1,0:T(8,128)(2,1)}, u32[]{:S(2)}, u32[]{:S(2)}) collective-permute-start(bf16[10,32,2048]{2,1,0:T(8,128)(2,1)} %collective-permute-done.27.refs_0_), channel_id=1, source_target_pairs={{0,1},{1,0},{2,3},{3,2},{4,5},{5,4},{6,7},{7,6},{8,9},{9,8},{10,11... | collective-permute-start | bytes 3932168 | tf_op jit(solution)/shard_map/ppermute | solution.py:243
  138.5 51.1 %collective-permute-start.30 = (bf16[10,32,2048]{2,1,0:T(8,128)(2,1)}, bf16[10,32,2048]{2,1,0:T(8,128)(2,1)}, u32[]{:S(2)}, u32[]{:S(2)}) collective-permute-start(bf16[10,32,2048]{2,1,0:T(8,128)(2,1)} %collective-permute-done.28.refs_1_), channel_id=1, source_target_pairs={{0,1},{1,0},{2,3},{3,2},{4,5},{5,4},{6,7},{7,6},{8,9},{9,8},{10,11... | collective-permute-start | bytes 3932168 | tf_op jit(solution)/shard_map/ppermute | solution.py:244
  192.0 35.3 %collective-permute-start.13 = (bf16[10,32,2048]{2,1,0:T(8,128)(2,1)}, bf16[10,32,2048]{2,1,0:T(8,128)(2,1)}, u32[]{:S(2)}, u32[]{:S(2)}) collective-permute-start(bf16[10,32,2048]{2,1,0:T(8,128)(2,1)} %gather_fusion.2), channel_id=1, source_target_pairs={{0,4},{4,0},{1,5},{5,1},{2,6},{6,2},{3,7},{7,3},{8,12},{12,8},{9,1... | collective-permute-start | bytes 3932168 | tf_op jit(solution)/shard_map/ppermute | solution.py:229
  194.3 54.6 %collective-permute-start.10 = (bf16[10,32,2048]{2,1,0:T(8,128)(2,1)S(1)}, bf16[10,32,2048]{2,1,0:T(8,128)(2,1)}, u32[]{:S(2)}, u32[]{:S(2)}) collective-permute-start(bf16[10,32,2048]{2,1,0:T(8,128)(2,1)S(1)} %gather_fusion.1), channel_id=1, source_target_pairs={{0,2},{2,0},{1,3},{3,1},{4,6},{6,4},{5,7},{7,5},{8,10},{10,8},{9,1... | collective-permute-start | bytes 3932168 | tf_op jit(solution)/shard_map/ppermute | solution.py:242
  199.2 55.8 %collective-permute-start.6 = (bf16[10,32,2048]{2,1,0:T(8,128)(2,1)}, bf16[10,32,2048]{2,1,0:T(8,128)(2,1)}, u32[]{:S(2)}, u32[]{:S(2)}) collective-permute-start(bf16[10,32,2048]{2,1,0:T(8,128)(2,1)} %gather_fusion), channel_id=1, source_target_pairs={{0,4},{4,0},{1,5},{5,1},{2,6},{6,2},{3,7},{7,3},{8,12},{12,8},{9,1... | collective-permute-start | bytes 3932168 | tf_op jit(solution)/shard_map/ppermute | solution.py:229
  224.3 39.6 %collective-permute-start.26 = (bf16[10,32,2048]{2,1,0:T(8,128)(2,1)}, bf16[10,32,2048]{2,1,0:T(8,128)(2,1)S(1)}, u32[]{:S(2)}, u32[]{:S(2)}) collective-permute-start(bf16[10,32,2048]{2,1,0:T(8,128)(2,1)} %collective-permute-done.24.refs_1_), channel_id=1, source_target_pairs={{0,1},{1,0},{2,3},{3,2},{4,5},{5,4},{6,7},{7,6},{8,9},{9,8},{10,11... | collective-permute-start | bytes 3932168 | tf_op jit(solution)/shard_map/ppermute | solution.py:244
  224.4 52.6 %collective-permute-start.21 = (bf16[10,32,2048]{2,1,0:T(8,128)(2,1)}, bf16[10,32,2048]{2,1,0:T(8,128)(2,1)}, u32[]{:S(2)}, u32[]{:S(2)}) collective-permute-start(bf16[10,32,2048]{2,1,0:T(8,128)(2,1)} %collective-permute-done.20.refs_0_), channel_id=1, source_target_pairs={{0,2},{2,0},{1,3},{3,1},{4,6},{6,4},{5,7},{7,5},{8,10},{10,8},{9,1... | collective-permute-start | bytes 3932168 | tf_op jit(solution)/shard_map/ppermute | solution.py:242
  227.3 50.0 %collective-permute-start.22 = (bf16[10,32,2048]{2,1,0:T(8,128)(2,1)}, bf16[10,32,2048]{2,1,0:T(8,128)(2,1)}, u32[]{:S(2)}, u32[]{:S(2)}) collective-permute-start(bf16[10,32,2048]{2,1,0:T(8,128)(2,1)} %collective-permute-done.20.refs_0_), channel_id=1, source_target_pairs={{0,1},{1,0},{2,3},{3,2},{4,5},{5,4},{6,7},{7,6},{8,9},{9,8},{10,11... | collective-permute-start | bytes 3932168 | tf_op jit(solution)/shard_map/ppermute | solution.py:243
  255.0 50.1 %collective-permute-start.14 = (bf16[10,32,2048]{2,1,0:T(8,128)(2,1)}, bf16[10,32,2048]{2,1,0:T(8,128)(2,1)}, u32[]{:S(2)}, u32[]{:S(2)}) collective-permute-start(bf16[10,32,2048]{2,1,0:T(8,128)(2,1)} %collective-permute-done.13.refs_0_), channel_id=1, source_target_pairs={{0,2},{2,0},{1,3},{3,1},{4,6},{6,4},{5,7},{7,5},{8,10},{10,8},{9,1... | collective-permute-start | bytes 3932168 | tf_op jit(solution)/shard_map/ppermute | solution.py:242
  265.1 60.2 %collective-permute-start.15 = (bf16[10,32,2048]{2,1,0:T(8,128)(2,1)}, bf16[10,32,2048]{2,1,0:T(8,128)(2,1)}, u32[]{:S(2)}, u32[]{:S(2)}) collective-permute-start(bf16[10,32,2048]{2,1,0:T(8,128)(2,1)} %collective-permute-done.13.refs_0_), channel_id=1, source_target_pairs={{0,1},{1,0},{2,3},{3,2},{4,5},{5,4},{6,7},{7,6},{8,9},{9,8},{10,11... | collective-permute-start | bytes 3932168 | tf_op jit(solution)/shard_map/ppermute | solution.py:243
  277.0 48.6 %collective-permute-start.23 = (bf16[10,32,2048]{2,1,0:T(8,128)(2,1)}, bf16[10,32,2048]{2,1,0:T(8,128)(2,1)}, u32[]{:S(2)}, u32[]{:S(2)}) collective-permute-start(bf16[10,32,2048]{2,1,0:T(8,128)(2,1)} %collective-permute-done.21.refs_1_), channel_id=1, source_target_pairs={{0,1},{1,0},{2,3},{3,2},{4,5},{5,4},{6,7},{7,6},{8,9},{9,8},{10,11... | collective-permute-start | bytes 3932168 | tf_op jit(solution)/shard_map/ppermute | solution.py:244
  277.3 120.3 %collective-permute-start.34 = (bf16[512,2048]{1,0:T(8,128)(2,1)}, bf16[512,2048]{1,0:T(8,128)(2,1)}, u32[]{:S(2)}, u32[]{:S(2)}) collective-permute-start(bf16[512,2048]{1,0:T(8,128)(2,1)} %param.9), channel_id=1, source_target_pairs={{0,2},{2,0},{1,3},{3,1},{4,6},{6,4},{5,7},{7,5},{8,10},{10,8},{9,1... | collective-permute-start | bytes 6291464 | tf_op jit(solution)/shard_map/ppermute | solution.py:250
  279.0 98.3 %collective-permute-start.7 = (bf16[10,32,2048]{2,1,0:T(8,128)(2,1)}, bf16[10,32,2048]{2,1,0:T(8,128)(2,1)S(1)}, u32[]{:S(2)}, u32[]{:S(2)}) collective-permute-start(bf16[10,32,2048]{2,1,0:T(8,128)(2,1)} %collective-permute-done.6.refs_0_), channel_id=1, source_target_pairs={{0,2},{2,0},{1,3},{3,1},{4,6},{6,4},{5,7},{7,5},{8,10},{10,8},{9,1... | collective-permute-start | bytes 3932168 | tf_op jit(solution)/shard_map/ppermute | solution.py:242
  305.1 72.2 %collective-permute-start.16 = (bf16[10,32,2048]{2,1,0:T(8,128)(2,1)}, bf16[10,32,2048]{2,1,0:T(8,128)(2,1)S(1)}, u32[]{:S(2)}, u32[]{:S(2)}) collective-permute-start(bf16[10,32,2048]{2,1,0:T(8,128)(2,1)} %collective-permute-done.14.refs_1_), channel_id=1, source_target_pairs={{0,1},{1,0},{2,3},{3,2},{4,5},{5,4},{6,7},{7,6},{8,9},{9,8},{10,11... | collective-permute-start | bytes 3932168 | tf_op jit(solution)/shard_map/ppermute | solution.py:244
  325.2 72.4 %collective-permute-start.11 = (bf16[10,32,2048]{2,1,0:T(8,128)(2,1)S(1)}, bf16[10,32,2048]{2,1,0:T(8,128)(2,1)S(1)}, u32[]{:S(2)}, u32[]{:S(2)}) collective-permute-start(bf16[10,32,2048]{2,1,0:T(8,128)(2,1)S(1)} %gather_fusion.1), channel_id=1, source_target_pairs={{0,1},{1,0},{2,3},{3,2},{4,5},{5,4},{6,7},{7,6},{8,9},{9,8},{10,11... | collective-permute-start | bytes 3932168 | tf_op jit(solution)/shard_map/ppermute | solution.py:243
  325.6 72.5 %collective-permute-start.12 = (bf16[10,32,2048]{2,1,0:T(8,128)(2,1)}, bf16[10,32,2048]{2,1,0:T(8,128)(2,1)S(1)}, u32[]{:S(2)}, u32[]{:S(2)}) collective-permute-start(bf16[10,32,2048]{2,1,0:T(8,128)(2,1)} %collective-permute-done.10.refs_1_), channel_id=1, source_target_pairs={{0,1},{1,0},{2,3},{3,2},{4,5},{5,4},{6,7},{7,6},{8,9},{9,8},{10,11... | collective-permute-start | bytes 3932168 | tf_op jit(solution)/shard_map/ppermute | solution.py:244
  397.6 58.1 %collective-permute-start.35 = (bf16[512,2048]{1,0:T(8,128)(2,1)}, bf16[512,2048]{1,0:T(8,128)(2,1)}, u32[]{:S(2)}, u32[]{:S(2)}) collective-permute-start(bf16[512,2048]{1,0:T(8,128)(2,1)} %param.9), channel_id=1, source_target_pairs={{0,1},{1,0},{2,3},{3,2},{4,5},{5,4},{6,7},{7,6},{8,9},{9,8},{10,11... | collective-permute-start | bytes 6291464 | tf_op jit(solution)/shard_map/ppermute | solution.py:251
  397.6 58.1 %collective-permute-start.36 = (bf16[512,2048]{1,0:T(8,128)(2,1)}, bf16[512,2048]{1,0:T(8,128)(2,1)}, u32[]{:S(2)}, u32[]{:S(2)}) collective-permute-start(bf16[512,2048]{1,0:T(8,128)(2,1)} %collective-permute-done.34), channel_id=1, source_target_pairs={{0,1},{1,0},{2,3},{3,2},{4,5},{5,4},{6,7},{7,6},{8,9},{9,8},{10,11... | collective-permute-start | bytes 6291464 | tf_op jit(solution)/shard_map/ppermute | solution.py:252
  (21 other events, 449.2 us)

commit v2 on v1

--- a/solution.py
+++ b/solution.py
@@ -101,12 +101,15 @@
     out[...] = product.astype(out.dtype).reshape(tiles, height, out.shape[2])
 
 
-def project(pieces, weight, slots, base, step, buffer):
-    tiles, depth = pieces[0].shape[0], pieces[0].shape[2]
-    width = weight.shape[1]
-    in_specs = [pl.BlockSpec((step, p.shape[1], depth), lambda i: (i, 0, 0)) for p in pieces]
+def project(pieces, tiles, weight, slots, base, step, buffer):
+    depth, width = weight.shape
+
+    def rows_from(array, start):
+        return pl.BlockSpec((step, array.shape[1], depth), lambda i: (start // step + i, 0, 0))
+
+    in_specs = [rows_from(*piece) for piece in pieces]
     in_specs.append(pl.BlockSpec((depth, width), lambda i: (0, 0)))
-    operands = list(pieces) + [weight]
+    operands = [array for array, _ in pieces] + [weight]
     aliases = {}
     if buffer is not None:
         aliases = {len(operands): 0}
@@ -183,6 +186,43 @@
     return chosen, jnp.sum(jnp.where(owned, rank, 0), axis=0)
 
 
+def pick_kernel(count, which, ids, *refs):
+    sources, outs, sems = refs[:count], refs[count:-1], refs[-1]
+    for at, source in enumerate(sources):
+
+        @pl.when(which[0] == at)
+        def _():
+            copies = []
+            for n, out in enumerate(outs):
+                for j in range(out.shape[0]):
+                    slot = n * out.shape[0] + j
+                    copies.append(
+                        pltpu.make_async_copy(source.at[ids[slot]], out.at[j], sems.at[slot])
+                    )
+            for copy in copies:
+                copy.start()
+            for copy in copies:
+                copy.wait()
+
+
+def pick(sources, which, lists):
+    capacity = lists[0].shape[0]
+    shape = jax.ShapeDtypeStruct((capacity,) + sources[0].shape[1:], sources[0].dtype)
+    size = capacity * len(lists) * sources[0].shape[1] * sources[0].shape[2]
+    return pl.pallas_call(
+        lambda *refs: pick_kernel(len(sources), *refs),
+        grid_spec=pltpu.PrefetchScalarGridSpec(
+            num_scalar_prefetch=2,
+            grid=(1,),
+            in_specs=[pl.BlockSpec(memory_space=pl.ANY)] * len(sources),
+            out_specs=[pl.BlockSpec(memory_space=pl.ANY)] * len(lists),
+            scratch_shapes=[pltpu.SemaphoreType.DMA((capacity * len(lists),))],
+        ),
+        out_shape=[shape] * len(lists),
+        cost_estimate=pl.CostEstimate(flops=0, bytes_accessed=4 * size, transcendentals=0),
+    )(which.reshape(1), jnp.concatenate(lists), *sources)
+
+
 def grid_body(tokens, norm_gain, in_weight, out_weight, pattern):
     shards = ZS * XS
     z, x = lax.axis_index("z"), lax.axis_index("x")
@@ -195,62 +235,89 @@
     head_width = in_weight.shape[2]
     share = TILE // PARTS
     order = jnp.asarray(ORDER, jnp.int32)[z]
+    step = capacity // 2
+
+    def line(up, down, s):
+        up = lax.ppermute(up, "z", [(i, i + 1) for i in range(s - 1, ZS - 1)])
+        down = lax.ppermute(down, "z", [(i, i - 1) for i in range(1, ZS - s + 1)])
+        return up, down
+
+    def across(a):
+        return lax.ppermute(a, "y", SWAP)
+
+    def aside(a):
+        return lax.ppermute(a, "c", SWAP)
+
+    def over(a):
+        return lax.ppermute(a, "x", SWAP)
 
     tiles = tokens.reshape(tile_count, PARTS, share, depth)
     mine = lax.dynamic_index_in_dim(tiles, y * CS + c, 1, keepdims=False)
     block = normalize(mine, norm_gain)
-
-    ups, downs = [block], [block]
-    for s in range(1, ZS):
-        ups.append(lax.ppermute(ups[-1], "z", [(i, i + 1) for i in range(s - 1, ZS - 1)]))
-        downs.append(lax.ppermute(downs[-1], "z", [(i, i - 1) for i in range(1, ZS - s + 1)]))
+    ups, downs = {}, {}
+    ups[1], downs[1] = line(block, block, 1)
 
     my_rows = lax.dynamic_slice_in_dim(pattern, me * tile_count, tile_count, 0)[:, 1:]
     beside_rows = lax.dynamic_slice_in_dim(pattern, beside * tile_count, tile_count, 0)[:, 1:]
     my_lists, my_rank = request_lists(my_rows, shards, tile_count, capacity)
     beside_lists, _ = request_lists(beside_rows, shards, tile_count, capacity)
 
-    def column_block(k):
-        parts = []
-        for at in range(ZS):
-            source = ORDER[at][k]
-            parts.append(ups[at - source] if source <= at else downs[source - at])
-        out = parts[0]
-        for at in range(1, ZS):
-            if parts[at] is not parts[at - 1]:
-                out = jnp.where(z >= at, parts[at], out)
-        return out
-
-    pieces = []
-    for k in range(ZS):
-        held = block if k == 0 else column_block(k)
-        source = order[k] * XS + x
-        out = held[beside_lists[source]]
-        came = lax.ppermute(out, "x", SWAP)
-        if k:
-            pieces.append(held[my_lists[source]])
-        pieces.append(came)
+    first = beside_lists[me] * PARTS + c
+    both = jnp.concatenate([first + y * CS, first + (1 - y) * CS])
+    rx0 = over(normalize(tokens.reshape(tile_count * PARTS, share, depth)[both], norm_gain))
+    w_across = across(out_weight)
 
     normed = normalize(tokens, norm_gain)
     queries = jnp.dot(
         normed, in_weight[:, 0, :], preferred_element_type=jnp.float32
     ).astype(jnp.bfloat16)
     weight = in_weight[:, 1:, :].reshape(depth, 2 * head_width)
-    slots = OWN_SLOTS + capacity * len(pieces)
-    buffer = project([normed.reshape(tile_count, TILE, depth)], weight, slots, 0, 4, None)
-    for at, piece in enumerate(pieces):
-        across = lax.ppermute(piece, "y", SWAP)
-        sides = lax.ppermute(piece, "c", SWAP)
-        corner = lax.ppermute(across, "c", SWAP)
-        buffer = project(
-            [piece, across, sides, corner], weight, slots,
-            OWN_SLOTS + at * capacity, capacity // 2, buffer,
-        )
-
-    w_across = lax.ppermute(out_weight, "y", SWAP)
-    w_sides = lax.ppermute(out_weight, "c", SWAP)
-    w_corner = lax.ppermute(w_across, "c", SWAP)
-    out_all = jnp.concatenate([out_weight, w_across, w_sides, w_corner], axis=0)
+    slots = OWN_SLOTS + capacity * (2 * ZS - 1)
+    buffer = project(
+        [(normed.reshape(tile_count, TILE, depth), 0)], tile_count, weight, slots, 0, 4, None
+    )
+
+    def after(lists, *results):
+        return lax.optimization_barrier((lists, results))[0]
+
+    def choose(k, lists, sources, which):
+        source = order[k] * XS + x
+        return pick(sources, which, [rows[source] for rows in lists])
+
+    def place(at, parts, buffer):
+        base = OWN_SLOTS + at * capacity
+        return project(parts, capacity, weight, slots, base, step, buffer)
+
+    def quarters(a, b):
+        return [(a, 0), (b, 0), (aside(a), 0), (aside(b), 0)]
+
+    lists = after((my_lists, beside_lists), ups[1], downs[1], buffer, queries, w_across)
+    ups[2], downs[2] = line(ups[1], downs[1], 2)
+    own1, out1 = choose(1, lists, [downs[1], ups[1]], z % 2)
+    rx1, own1y = over(out1), across(own1)
+    side0 = aside(rx0)
+    buffer = place(
+        0, [(rx0, 0), (rx0, capacity), (side0, 0), (side0, capacity)], buffer
+    )
+
+    lists = after(lists, ups[2], downs[2], rx1, own1y, buffer)
+    ups[3], downs[3] = line(ups[2], downs[2], 3)
+    own2, out2 = choose(2, lists, [downs[2], downs[1], ups[1], ups[2]], z)
+    rx1y, rx2, own2y = across(rx1), over(out2), across(own2)
+    buffer = place(1, quarters(own1, own1y), buffer)
+    buffer = place(2, quarters(rx1, rx1y), buffer)
+
+    lists = after(lists, ups[3], downs[3], rx2, own2y, buffer)
+    own3, out3 = choose(3, lists, [downs[3], downs[2], ups[2], ups[3]], z)
+    rx2y, rx3, own3y = across(rx2), over(out3), across(own3)
+    buffer = place(3, quarters(own2, own2y), buffer)
+    buffer = place(4, quarters(rx2, rx2y), buffer)
+    rx3y = across(rx3)
+    buffer = place(5, quarters(own3, own3y), buffer)
+    buffer = place(6, quarters(rx3, rx3y), buffer)
+    out_all = jnp.concatenate(
+        [out_weight, w_across, aside(out_weight), aside(w_across)], axis=0
+    )
 
     owner = my_rows // tile_count
     step_of = jnp.sum(
@@ -261,8 +328,8 @@
         ),
         axis=2,
     )
-    place = 2 * step_of - jnp.where(owner % XS == x, 1, 0)
-    far_slots = OWN_SLOTS + place * capacity + my_rank.reshape(tile_count, KT - 1)
+    group = 2 * step_of - jnp.where(owner % XS == x, 1, 0)
+    far_slots = OWN_SLOTS + group * capacity + my_rank.reshape(tile_count, KT - 1)
     slot_ids = jnp.concatenate(
         [jnp.arange(tile_count, dtype=jnp.int32)[:, None], far_slots], axis=1
     )
@@ -275,14 +342,12 @@
         picked = lax.dynamic_slice_in_dim(slot_ids, which * half, half, 0)
         return attend(ids, picked.reshape(-1), queries, buffer)
 
-    far = attend_half(1 - y)
-    far_came = lax.ppermute(far, "y", SWAP)
+    far_came = across(attend_half(1 - y))
     own = attend_half(y)
     quarter = own.shape[0] // CS
     keep = [lax.dynamic_slice_in_dim(a, c * quarter, quarter, 0) for a in (own, far_came)]
     give = [lax.dynamic_slice_in_dim(a, (1 - c) * quarter, quarter, 0) for a in (own, far_came)]
-    came = [lax.ppermute(a, "c", SWAP) for a in give]
-    attended = jnp.concatenate(keep + came, axis=1)
+    attended = jnp.concatenate(keep + [aside(a) for a in give], axis=1)
     return jnp.dot(attended, out_all, preferred_element_type=jnp.float32).astype(jnp.bfloat16)
 
 

time: 466 us -> 604 us (1.30)
  Pallas kernels: 105 us -> 349 us
  waiting for transfers between devices: 250 us -> 157 us
  local copies, waits for them, and re-layouts: 33.7 us -> 24.1 us
    pallas_call x0 -> x3, Pallas kernels: none -> 244 us  [pick(): pl.pallas_call(lambda *refs: pick_kernel(len(sources), *refs), grid_spec=...]
    ppermute x37 -> x35, waiting for transfers between devices: 250 us -> 157 us  [the longest x8 72.7 us: across(): return lax.ppermute(a, 'y', SWAP)]
    gather x7 -> x1, local copies, waits for them, and re-layouts: 15.8 us -> 4.1 us  [grid_body(): tokens.reshape(tile_count * PARTS, share, depth)[both]]
    select_n x9 -> x2, other arithmetic: 6.5 us -> 0.09 us  [the longest x1 0.08 us: grid_body(): tokens.reshape(tile_count * PARTS, share, depth)[both]]
    ppermute x37 -> x35, starting transfers between devices: 32.4 us -> 27.8 us  [the longest x3 10.3 us: line(): up = lax.ppermute(up, 'z', [(i, i + 1) for i in range(s - 1, ZS - 1)])]
    convert_element_type x2 -> x3, other arithmetic: 10.8 us -> 14.2 us  [normalize(): (values * lax.rsqrt(mean_square + 1e-05) * norm_gain).astype(jnp.bfloat16)]
  transfers between devices with their start and end apart: 37 -> 35, of which waited for: 15 -> 13; matrix products, arithmetic and copies ran while one was open for 13% -> 8% of each run, Pallas kernels for 23% -> 58%
where the time goes in v2:
time: 604 us; the launch traced here: 601 us
  Pallas kernels  349 us (58%)
  waiting for transfers between devices  157 us (26%)
  starting transfers between devices  27.8 us (5%)
  other arithmetic  25.2 us (4%)
  local copies, waits for them, and re-layouts  24.1 us (4%)
  matrix products  15.1 us (2%)
    pallas_call x3, Pallas kernels, pick(): pl.pallas_call(lambda *refs: pick_kernel(len(sources), *refs), grid_spec=...  244 us
    pallas_call x8, Pallas kernels, project(): pl.pallas_call(lambda *refs: project_kernel(len(pieces), *refs), grid=(ti...  80.9 us
    ppermute x8, waiting for transfers between devices, across(): return lax.ppermute(a, 'y', SWAP)  72.7 us
    ppermute x4, waiting for transfers between devices, over(): return lax.ppermute(a, 'x', SWAP)  59.5 us
    pallas_call x2, Pallas kernels, attend(): pl.pallas_call(attend_kernel, grid_spec=pltpu.PrefetchScalarGridSpec(num_...  23.9 us
    ppermute x3, waiting for transfers between devices, line(): down = lax.ppermute(down, 'z', [(i, i - 1) for i in range(1, ZS - s + 1)])  20.9 us
    convert_element_type x3, other arithmetic, normalize(): (values * lax.rsqrt(mean_square + 1e-05) * norm_gain).astype(jnp.bfloat16)  14.2 us
  transfers between devices with their start and end apart: 35, of which 13 were waited for; matrix products, arithmetic and copies ran while one was open for 8% of the time, Pallas kernels for 58%

profile of v2, /device:TPU:0, one launch (start us, length us, event | category | flops | bytes accessed | tf_op | source)
XLA Modules:
  0.0 600.6 jit_solution(9952739617482461039)
XLA Ops:
  5.6 6.3 %collective-permute-start = (bf16[16,32,2048]{2,1,0:T(8,128)(2,1)}, bf16[16,32,2048]{2,1,0:T(8,128)(2,1)}, u32[]{:S(2)}, u32[]{:S(2)}) collective-permute-start(bf16[16,32,2048]{2,1,0:T(8,128)(2,1)} %fusion.16), channel_id=1, source_target_pairs={{0,8},{8,16},{16,24},{1,9},{9,17},{17,25},{2,10},{10,18},{18,26},{... | collective-permute-start | bytes 6291464 | tf_op jit(solution)/shard_map/ppermute | solution.py:241
  34.1 8.6 %fusion.2 = bf16[2048,2048]{1,0:T(8,128)(2,1)} fusion(bf16[2048,2048]{1,0:T(8,128)(2,1)} %param.6, f32[2048]{0:T(1024)S(1)} %copy-done.8, f32[2048]{0:T(1024)S(1)} %add_rsqrt_fusion.2), kind=kLoop, calls=%fused_computation.5 | loop fusion | flops 16777216 | bytes 16793600 | tf_op jit(solution)/shard_map/convert_element_type | solution.py:25
  52.0 12.2 %shard_map.64.refs_5_ = bf16[90,128,1024]{2,1,0:T(8,128)(2,1)} custom-call(bf16[16,128,2048]{2,1,0:T(8,128)(2,1)} %bitcast.38, bf16[2048,1024]{1,0:T(8,128)(2,1)S(1)} %bitcast.34), custom_call_target="tpu_custom_call" | custom-call | flops 8589934592 | bytes 16777216 | tf_op jit(solution)/shard_map/pallas_call | solution.py:119
  64.3 7.2 %convolution_convert_fusion.query = bf16[2048,512]{1,0:T(8,128)(2,1)} fusion(bf16[2048,2048]{1,0:T(8,128)(2,1)S(1)} %copy-done.7, bf16[2048,3,512]{2,0,1:T(8,128)(2,1)} %param.8), kind=kOutput, calls=%fused_computation.26 | convolution fusion | flops 4296015872 | bytes 12582912 | tf_op jit(solution)/shard_map/dot_general | solution.py:271
  72.5 81.4 %shard_map.65 = (bf16[10,32,2048]{2,1,0:T(8,128)(2,1)}, bf16[10,32,2048]{2,1,0:T(8,128)(2,1)}) custom-call(s32[1]{0:T(128)} %bitcast.7.refs_0_, s32[20]{0:T(128)} %pad_add_fusion.1.refs_1_, bf16[16,32,2048]{2,1,0:T(8,128)(2,1)} %collective-permute-done.1.refs_2_.refs_3_, bf16[16,32,2048]{2,1,0:T(8,128)(2,1)} %collective-permute-done.refs_3_.refs_4_), custom_call_target="tpu_custom_call" | custom-call | bytes 5242880 | tf_op jit(solution)/shard_map/pallas_call | solution.py:212
  158.4 25.5 %collective-permute-done.5.refs_0_ = bf16[10,32,2048]{2,1,0:T(8,128)(2,1)} collective-permute-done((bf16[10,32,2048]{2,1,0:T(8,128)(2,1)}, bf16[10,32,2048]{2,1,0:T(8,128)(2,1)}, u32[]{:S(2)}, u32[]{:S(2)}) %collective-permute-start.5) | collective-permute-done | bytes 1310752 | tf_op jit(solution)/shard_map/ppermute | solution.py:252
  188.8 20.8 %collective-permute-done.4.refs_2_.refs_3_ = bf16[16,32,2048]{2,1,0:T(8,128)(2,1)} collective-permute-done((bf16[16,32,2048]{2,1,0:T(8,128)(2,1)}, bf16[16,32,2048]{2,1,0:T(8,128)(2,1)}, u32[]{:S(2)}, u32[]{:S(2)}) %collective-permute-start.4) | collective-permute-done | bytes 2097184 | tf_op jit(solution)/shard_map/ppermute | solution.py:242
  218.2 9.5 %shard_map.66.refs_5_ = bf16[90,128,1024]{2,1,0:T(8,128)(2,1)} custom-call(bf16[20,32,2048]{2,1,0:T(8,128)(2,1)S(1)} %collective-permute-done.7.refs_0_.refs_1_, bf16[20,32,2048]{2,1,0:T(8,128)(2,1)S(1)} %collective-permute-done.7.refs_0_.refs_1_, bf16[20,32,2048]{2,1,0:T(8,128)(2,1)} %collective-permute-done.8.refs_2_.refs_3_, ...), custom_call_target="tpu_custom_call", output_to_operand_aliasing={{}: (5, {})} | custom-call | flops 5368709120 | bytes 12058624 | tf_op jit(solution)/shard_map/pallas_call | solution.py:119
  228.7 81.4 %shard_map.67 = (bf16[10,32,2048]{2,1,0:T(8,128)(2,1)}, bf16[10,32,2048]{2,1,0:T(8,128)(2,1)}) custom-call(s32[1]{0:T(128)} %bitcast.2.refs_0_, s32[20]{0:T(128)} %pad_add_fusion.2.refs_1_, bf16[16,32,2048]{2,1,0:T(8,128)(2,1)} %collective-permute-done.4.refs_2_.refs_3_, bf16[16,32,2048]{2,1,0:T(8,128)(2,1)} %collective-permute-done.1.refs_2_.refs_3_, ...), custom_call_target="tpu_custom_call" | custom-call | bytes 5242880 | tf_op jit(solution)/shard_map/pallas_call | solution.py:212
  314.5 9.5 %shard_map.68.refs_5_ = bf16[90,128,1024]{2,1,0:T(8,128)(2,1)} custom-call(bf16[10,32,2048]{2,1,0:T(8,128)(2,1)S(1)} %copy-done.4, bf16[10,32,2048]{2,1,0:T(8,128)(2,1)} %collective-permute-done.6.refs_1_, bf16[10,32,2048]{2,1,0:T(8,128)(2,1)S(1)} %copy-done.6, ...), custom_call_target="tpu_custom_call", output_to_operand_aliasing={{}: (5, {})} | custom-call | flops 5368709120 | bytes 12058624 | tf_op jit(solution)/shard_map/pallas_call | solution.py:119
  324.1 10.1 %shard_map.69.refs_5_ = bf16[90,128,1024]{2,1,0:T(8,128)(2,1)} custom-call(bf16[10,32,2048]{2,1,0:T(8,128)(2,1)} %collective-permute-done.5.refs_0_, bf16[10,32,2048]{2,1,0:T(8,128)(2,1)} %collective-permute-done.13.refs_1_, bf16[10,32,2048]{2,1,0:T(8,128)(2,1)} %collective-permute-done.14.refs_2_, ...), custom_call_target="tpu_custom_call", output_to_operand_aliasing={{}: (5, {})} | custom-call | flops 5368709120 | bytes 12058624 | tf_op jit(solution)/shard_map/pallas_call | solution.py:119
  334.2 7.3 %collective-permute-done.11.refs_0_ = bf16[10,32,2048]{2,1,0:T(8,128)(2,1)S(1)} collective-permute-done((bf16[10,32,2048]{2,1,0:T(8,128)(2,1)}, bf16[10,32,2048]{2,1,0:T(8,128)(2,1)S(1)}, u32[]{:S(2)}, u32[]{:S(2)}) %collective-permute-start.11) | collective-permute-done | bytes 1310752 | tf_op jit(solution)/shard_map/ppermute | solution.py:252
  342.8 81.4 %shard_map.70 = (bf16[10,32,2048]{2,1,0:T(8,128)(2,1)}, bf16[10,32,2048]{2,1,0:T(8,128)(2,1)}) custom-call(s32[1]{0:T(128)} %bitcast.2.refs_0_, s32[20]{0:T(128)} %pad_add_fusion.3.refs_1_, bf16[16,32,2048]{2,1,0:T(8,128)(2,1)} %collective-permute-done.10.refs_2_, bf16[16,32,2048]{2,1,0:T(8,128)(2,1)} %collective-permute-done.4.refs_2_.refs_3_, ...), custom_call_target="tpu_custom_call" | custom-call | bytes 5242880 | tf_op jit(solution)/shard_map/pallas_call | solution.py:212
  428.0 26.7 %collective-permute-done.18.refs_0_ = bf16[10,32,2048]{2,1,0:T(8,128)(2,1)} collective-permute-done((bf16[10,32,2048]{2,1,0:T(8,128)(2,1)}, bf16[10,32,2048]{2,1,0:T(8,128)(2,1)}, u32[]{:S(2)}, u32[]{:S(2)}) %collective-permute-start.18) | collective-permute-done | bytes 1310752 | tf_op jit(solution)/shard_map/ppermute | solution.py:252
  458.4 27.2 %collective-permute-done.22.refs_1_ = bf16[10,32,2048]{2,1,0:T(8,128)(2,1)} collective-permute-done((bf16[10,32,2048]{2,1,0:T(8,128)(2,1)}, bf16[10,32,2048]{2,1,0:T(8,128)(2,1)}, u32[]{:S(2)}, u32[]{:S(2)}) %collective-permute-start.22) | collective-permute-done | bytes 1310752 | tf_op jit(solution)/shard_map/ppermute | solution.py:246
  486.5 25.3 %collective-permute-done.19.refs_1_ = bf16[10,32,2048]{2,1,0:T(8,128)(2,1)} collective-permute-done((bf16[10,32,2048]{2,1,0:T(8,128)(2,1)}, bf16[10,32,2048]{2,1,0:T(8,128)(2,1)}, u32[]{:S(2)}, u32[]{:S(2)}) %collective-permute-start.19) | collective-permute-done | bytes 1310752 | tf_op jit(solution)/shard_map/ppermute | solution.py:246
  511.8 9.8 %shard_map.71.refs_5_ = bf16[90,128,1024]{2,1,0:T(8,128)(2,1)} custom-call(bf16[10,32,2048]{2,1,0:T(8,128)(2,1)S(1)} %copy-done.2, bf16[10,32,2048]{2,1,0:T(8,128)(2,1)} %collective-permute-done.12.refs_1_, bf16[10,32,2048]{2,1,0:T(8,128)(2,1)} %collective-permute-done.28.refs_2_, ...), custom_call_target="tpu_custom_call", output_to_operand_aliasing={{}: (5, {})} | custom-call | flops 5368709120 | bytes 12058624 | tf_op jit(solution)/shard_map/pallas_call | solution.py:119
  522.2 9.9 %shard_map.72.refs_5_ = bf16[90,128,1024]{2,1,0:T(8,128)(2,1)} custom-call(bf16[10,32,2048]{2,1,0:T(8,128)(2,1)S(1)} %collective-permute-done.11.refs_0_, bf16[10,32,2048]{2,1,0:T(8,128)(2,1)} %collective-permute-done.25.refs_1_, bf16[10,32,2048]{2,1,0:T(8,128)(2,1)} %collective-permute-done.26.refs_2_, ...), custom_call_target="tpu_custom_call", output_to_operand_aliasing={{}: (5, {})} | custom-call | flops 5368709120 | bytes 12058624 | tf_op jit(solution)/shard_map/pallas_call | solution.py:119
  532.2 10.1 %shard_map.73.refs_5_ = bf16[90,128,1024]{2,1,0:T(8,128)(2,1)} custom-call(bf16[10,32,2048]{2,1,0:T(8,128)(2,1)S(1)} %copy-done.3, bf16[10,32,2048]{2,1,0:T(8,128)(2,1)} %collective-permute-done.22.refs_1_, bf16[10,32,2048]{2,1,0:T(8,128)(2,1)} %collective-permute-done.23.refs_2_, ...), custom_call_target="tpu_custom_call", output_to_operand_aliasing={{}: (5, {})} | custom-call | flops 5368709120 | bytes 12058624 | tf_op jit(solution)/shard_map/pallas_call | solution.py:119
  542.3 9.7 %shard_map.74.refs_0_.refs_1_.refs_2_.refs_3_ = bf16[90,128,1024]{2,1,0:T(8,128)(2,1)} custom-call(bf16[10,32,2048]{2,1,0:T(8,128)(2,1)} %collective-permute-done.18.refs_0_, bf16[10,32,2048]{2,1,0:T(8,128)(2,1)} %collective-permute-done.19.refs_1_, bf16[10,32,2048]{2,1,0:T(8,128)(2,1)S(1)} %collective-permute-done.20.refs_2_, ...), custom_call_target="tpu_custom_call", output_to_operand_aliasing={{}: (5, {})} | custom-call | flops 5368709120 | bytes 12058624 | tf_op jit(solution)/shard_map/pallas_call | solution.py:119
  552.0 12.0 %shard_map.76 = bf16[1024,512]{1,0:T(8,128)(2,1)S(1)} custom-call(s32[8]{0:T(128)S(1)} %iota_add_fusion.tile_ids, s32[32]{0:T(128)S(1)} %reshape.322.slot_ids, bf16[2048,512]{1,0:T(8,128)(2,1)S(1)} %copy-done.1, bf16[90,128,1024]{2,1,0:T(8,128)(2,1)} %shard_map.74.refs_0_.refs_1_.refs_2_.refs_3_, ...), custom_call_target="tpu_custom_call" | custom-call | flops 1073741824 | bytes 10485760 | tf_op jit(solution)/shard_map/pallas_call | solution.py:160
  564.7 11.9 %shard_map.75 = bf16[1024,512]{1,0:T(8,128)(2,1)S(1)} custom-call(s32[8]{0:T(128)S(1)} %iota_add_fusion.1.tile_ids, s32[32]{0:T(128)S(1)} %reshape.314.slot_ids, bf16[2048,512]{1,0:T(8,128)(2,1)S(1)} %copy-done.1, bf16[90,128,1024]{2,1,0:T(8,128)(2,1)} %shard_map.74.refs_0_.refs_1_.refs_2_.refs_3_, ...), custom_call_target="tpu_custom_call" | custom-call | flops 1073741824 | bytes 10485760 | tf_op jit(solution)/shard_map/pallas_call | solution.py:160
  576.9 12.6 %collective-permute-done.30 = bf16[1024,512]{1,0:T(8,128)(2,1)} collective-permute-done((bf16[1024,512]{1,0:T(8,128)(2,1)S(1)}, bf16[1024,512]{1,0:T(8,128)(2,1)}, u32[]{:S(2)}, u32[]{:S(2)}) %collective-permute-start.30) | collective-permute-done | bytes 1048608 | tf_op jit(solution)/shard_map/ppermute | solution.py:246
  592.8 7.8 %fusion.17 = bf16[512,2048]{1,0:T(8,128)(2,1)} fusion(bf16[512,2048]{1,0:T(8,128)(2,1)} %collective-permute-done.34, bf16[512,2048]{1,0:T(8,128)(2,1)} %collective-permute-done.33, bf16[512,2048]{1,0:T(8,128)(2,1)} %collective-permute-done.2, bf16[512,2048]{1,0:T(8,128)(2,1)} %param.9, bf16[512,512]{1,0:T(8,128)(2,1)S(1)} %collective-permute-done.32, ...), kind=kOutput, calls=%fused_computation.25 | convolution fusion | flops 4337958912 | bytes 12582912 | tf_op jit(solution)/shard_map/dot_general | solution.py:351
  (138 shorter events, 74.2 us)
Async XLA Ops:
  5.6 65.9 %collective-permute-start = (bf16[16,32,2048]{2,1,0:T(8,128)(2,1)}, bf16[16,32,2048]{2,1,0:T(8,128)(2,1)}, u32[]{:S(2)}, u32[]{:S(2)}) collective-permute-start(bf16[16,32,2048]{2,1,0:T(8,128)(2,1)} %fusion.16), channel_id=1, source_target_pairs={{0,8},{8,16},{16,24},{1,9},{9,17},{17,25},{2,10},{10,18},{18,26},{... | collective-permute-start | bytes 6291464 | tf_op jit(solution)/shard_map/ppermute | solution.py:241
  11.8 59.7 %collective-permute-start.1 = (bf16[16,32,2048]{2,1,0:T(8,128)(2,1)}, bf16[16,32,2048]{2,1,0:T(8,128)(2,1)}, u32[]{:S(2)}, u32[]{:S(2)}) collective-permute-start(bf16[16,32,2048]{2,1,0:T(8,128)(2,1)} %fusion.16), channel_id=1, source_target_pairs={{8,0},{16,8},{24,16},{9,1},{17,9},{25,17},{10,2},{18,10},{26,18},{... | collective-permute-start | bytes 6291464 | tf_op jit(solution)/shard_map/ppermute | solution.py:242
  13.1 58.4 %collective-permute-start.2 = (bf16[512,2048]{1,0:T(8,128)(2,1)}, bf16[512,2048]{1,0:T(8,128)(2,1)}, u32[]{:S(2)}, u32[]{:S(2)}) collective-permute-start(bf16[512,2048]{1,0:T(8,128)(2,1)} %param.9), channel_id=1, source_target_pairs={{0,2},{2,0},{1,3},{3,1},{4,6},{6,4},{5,7},{7,5},{8,10},{10,8},{9,1... | collective-permute-start | bytes 6291464 | tf_op jit(solution)/shard_map/ppermute | solution.py:246
  22.9 134.1 %collective-permute-start.7 = (bf16[20,32,2048]{2,1,0:T(8,128)(2,1)}, bf16[20,32,2048]{2,1,0:T(8,128)(2,1)S(1)}, u32[]{:S(2)}, u32[]{:S(2)}) collective-permute-start(bf16[20,32,2048]{2,1,0:T(8,128)(2,1)} %fusion.13), channel_id=1, source_target_pairs={{0,4},{4,0},{1,5},{5,1},{2,6},{6,2},{3,7},{7,3},{8,12},{12,8},{9,1... | collective-permute-start | bytes 7864328 | tf_op jit(solution)/shard_map/ppermute | solution.py:252
  155.0 33.4 %collective-permute-start.3 = (bf16[16,32,2048]{2,1,0:T(8,128)(2,1)}, bf16[16,32,2048]{2,1,0:T(8,128)(2,1)}, u32[]{:S(2)}, u32[]{:S(2)}) collective-permute-start(bf16[16,32,2048]{2,1,0:T(8,128)(2,1)} %collective-permute-done.refs_3_.refs_4_), channel_id=1, source_target_pairs={{8,16},{16,24},{9,17},{17,25},{10,18},{18,26},{11,19},{19,27},{12,... | collective-permute-start | bytes 6291464 | tf_op jit(solution)/shard_map/ppermute | solution.py:241
  157.0 61.1 %collective-permute-start.8 = (bf16[20,32,2048]{2,1,0:T(8,128)(2,1)S(1)}, bf16[20,32,2048]{2,1,0:T(8,128)(2,1)}, u32[]{:S(2)}, u32[]{:S(2)}) collective-permute-start(bf16[20,32,2048]{2,1,0:T(8,128)(2,1)S(1)} %collective-permute-done.7.refs_0_.refs_1_), channel_id=1, source_target_pairs={{0,1},{1,0},{2,3},{3,2},{4,5},{5,4},{6,7},{7,6},{8,9},{9,8},{10,11... | collective-permute-start | bytes 7864328 | tf_op jit(solution)/shard_map/ppermute | solution.py:249
  157.0 52.6 %collective-permute-start.4 = (bf16[16,32,2048]{2,1,0:T(8,128)(2,1)}, bf16[16,32,2048]{2,1,0:T(8,128)(2,1)}, u32[]{:S(2)}, u32[]{:S(2)}) collective-permute-start(bf16[16,32,2048]{2,1,0:T(8,128)(2,1)} %collective-permute-done.1.refs_2_.refs_3_), channel_id=1, source_target_pairs={{8,0},{16,8},{9,1},{17,9},{10,2},{18,10},{11,3},{19,11},{12,4},{20... | collective-permute-start | bytes 6291464 | tf_op jit(solution)/shard_map/ppermute | solution.py:242
  188.3 121.8 %collective-permute-start.17 = (bf16[10,32,2048]{2,1,0:T(8,128)(2,1)}, bf16[10,32,2048]{2,1,0:T(8,128)(2,1)}, u32[]{:S(2)}, u32[]{:S(2)}) collective-permute-start(bf16[10,32,2048]{2,1,0:T(8,128)(2,1)} %collective-permute-done.6.refs_1_), channel_id=1, source_target_pairs={{0,1},{1,0},{2,3},{3,2},{4,5},{5,4},{6,7},{7,6},{8,9},{9,8},{10,11... | collective-permute-start | bytes 3932168 | tf_op jit(solution)/shard_map/ppermute | solution.py:249
  188.4 122.2 %collective-permute-start.14 = (bf16[10,32,2048]{2,1,0:T(8,128)(2,1)}, bf16[10,32,2048]{2,1,0:T(8,128)(2,1)}, u32[]{:S(2)}, u32[]{:S(2)}) collective-permute-start(bf16[10,32,2048]{2,1,0:T(8,128)(2,1)} %collective-permute-done.5.refs_0_), channel_id=1, source_target_pairs={{0,1},{1,0},{2,3},{3,2},{4,5},{5,4},{6,7},{7,6},{8,9},{9,8},{10,11... | collective-permute-start | bytes 3932168 | tf_op jit(solution)/shard_map/ppermute | solution.py:249
  209.6 124.6 %collective-permute-start.10 = (bf16[16,32,2048]{2,1,0:T(8,128)(2,1)}, bf16[16,32,2048]{2,1,0:T(8,128)(2,1)}, u32[]{:S(2)}, u32[]{:S(2)}) collective-permute-start(bf16[16,32,2048]{2,1,0:T(8,128)(2,1)} %collective-permute-done.4.refs_2_.refs_3_), channel_id=1, source_target_pairs={{8,0},{9,1},{10,2},{11,3},{12,4},{13,5},{14,6},{15,7}} | collective-permute-start | bytes 6291464 | tf_op jit(solution)/shard_map/ppermute | solution.py:242
  215.5 118.7 %collective-permute-start.9 = (bf16[16,32,2048]{2,1,0:T(8,128)(2,1)}, bf16[16,32,2048]{2,1,0:T(8,128)(2,1)}, u32[]{:S(2)}, u32[]{:S(2)}) collective-permute-start(bf16[16,32,2048]{2,1,0:T(8,128)(2,1)} %collective-permute-done.3.refs_5_.refs_4_), channel_id=1, source_target_pairs={{16,24},{17,25},{18,26},{19,27},{20,28},{21,29},{22,30},{23,31}} | collective-permute-start | bytes 6291464 | tf_op jit(solution)/shard_map/ppermute | solution.py:241
  218.1 105.9 %collective-permute-start.15 = (bf16[10,32,2048]{2,1,0:T(8,128)(2,1)}, bf16[10,32,2048]{2,1,0:T(8,128)(2,1)}, u32[]{:S(2)}, u32[]{:S(2)}) collective-permute-start(bf16[10,32,2048]{2,1,0:T(8,128)(2,1)} %collective-permute-done.13.refs_1_), channel_id=1, source_target_pairs={{0,1},{1,0},{2,3},{3,2},{4,5},{5,4},{6,7},{7,6},{8,9},{9,8},{10,11... | collective-permute-start | bytes 3932168 | tf_op jit(solution)/shard_map/ppermute | solution.py:249
  324.0 103.7 %collective-permute-start.28 = (bf16[10,32,2048]{2,1,0:T(8,128)(2,1)S(1)}, bf16[10,32,2048]{2,1,0:T(8,128)(2,1)}, u32[]{:S(2)}, u32[]{:S(2)}) collective-permute-start(bf16[10,32,2048]{2,1,0:T(8,128)(2,1)S(1)} %copy-done.2), channel_id=1, source_target_pairs={{0,1},{1,0},{2,3},{3,2},{4,5},{5,4},{6,7},{7,6},{8,9},{9,8},{10,11... | collective-permute-start | bytes 3932168 | tf_op jit(solution)/shard_map/ppermute | solution.py:249
  425.7 31.8 %collective-permute-start.25 = (bf16[10,32,2048]{2,1,0:T(8,128)(2,1)S(1)}, bf16[10,32,2048]{2,1,0:T(8,128)(2,1)}, u32[]{:S(2)}, u32[]{:S(2)}) collective-permute-start(bf16[10,32,2048]{2,1,0:T(8,128)(2,1)S(1)} %collective-permute-done.11.refs_0_), channel_id=1, source_target_pairs={{0,2},{2,0},{1,3},{3,1},{4,6},{6,4},{5,7},{7,5},{8,10},{10,8},{9,1... | collective-permute-start | bytes 3932168 | tf_op jit(solution)/shard_map/ppermute | solution.py:246
  426.2 31.6 %collective-permute-start.29 = (bf16[10,32,2048]{2,1,0:T(8,128)(2,1)}, bf16[10,32,2048]{2,1,0:T(8,128)(2,1)}, u32[]{:S(2)}, u32[]{:S(2)}) collective-permute-start(bf16[10,32,2048]{2,1,0:T(8,128)(2,1)} %collective-permute-done.12.refs_1_), channel_id=1, source_target_pairs={{0,1},{1,0},{2,3},{3,2},{4,5},{5,4},{6,7},{7,6},{8,9},{9,8},{10,11... | collective-permute-start | bytes 3932168 | tf_op jit(solution)/shard_map/ppermute | solution.py:249
  426.2 59.4 %collective-permute-start.22 = (bf16[10,32,2048]{2,1,0:T(8,128)(2,1)}, bf16[10,32,2048]{2,1,0:T(8,128)(2,1)}, u32[]{:S(2)}, u32[]{:S(2)}) collective-permute-start(bf16[10,32,2048]{2,1,0:T(8,128)(2,1)} %get-tuple-element.28.refs_0_), channel_id=1, source_target_pairs={{0,2},{2,0},{1,3},{3,1},{4,6},{6,4},{5,7},{7,5},{8,10},{10,8},{9,1... | collective-permute-start | bytes 3932168 | tf_op jit(solution)/shard_map/ppermute | solution.py:246
  427.7 58.1 %collective-permute-start.26 = (bf16[10,32,2048]{2,1,0:T(8,128)(2,1)S(1)}, bf16[10,32,2048]{2,1,0:T(8,128)(2,1)}, u32[]{:S(2)}, u32[]{:S(2)}) collective-permute-start(bf16[10,32,2048]{2,1,0:T(8,128)(2,1)S(1)} %collective-permute-done.11.refs_0_), channel_id=1, source_target_pairs={{0,1},{1,0},{2,3},{3,2},{4,5},{5,4},{6,7},{7,6},{8,9},{9,8},{10,11... | collective-permute-start | bytes 3932168 | tf_op jit(solution)/shard_map/ppermute | solution.py:249
  454.6 57.1 %collective-permute-start.19 = (bf16[10,32,2048]{2,1,0:T(8,128)(2,1)}, bf16[10,32,2048]{2,1,0:T(8,128)(2,1)}, u32[]{:S(2)}, u32[]{:S(2)}) collective-permute-start(bf16[10,32,2048]{2,1,0:T(8,128)(2,1)} %collective-permute-done.18.refs_0_), channel_id=1, source_target_pairs={{0,2},{2,0},{1,3},{3,1},{4,6},{6,4},{5,7},{7,5},{8,10},{10,8},{9,1... | collective-permute-start | bytes 3932168 | tf_op jit(solution)/shard_map/ppermute | solution.py:246
  457.5 64.1 %collective-permute-start.27 = (bf16[10,32,2048]{2,1,0:T(8,128)(2,1)}, bf16[10,32,2048]{2,1,0:T(8,128)(2,1)}, u32[]{:S(2)}, u32[]{:S(2)}) collective-permute-start(bf16[10,32,2048]{2,1,0:T(8,128)(2,1)} %collective-permute-done.25.refs_1_), channel_id=1, source_target_pairs={{0,1},{1,0},{2,3},{3,2},{4,5},{5,4},{6,7},{7,6},{8,9},{9,8},{10,11... | collective-permute-start | bytes 3932168 | tf_op jit(solution)/shard_map/ppermute | solution.py:249
  457.8 74.2 %collective-permute-start.23 = (bf16[10,32,2048]{2,1,0:T(8,128)(2,1)}, bf16[10,32,2048]{2,1,0:T(8,128)(2,1)}, u32[]{:S(2)}, u32[]{:S(2)}) collective-permute-start(bf16[10,32,2048]{2,1,0:T(8,128)(2,1)} %get-tuple-element.28.refs_0_), channel_id=1, source_target_pairs={{0,1},{1,0},{2,3},{3,2},{4,5},{5,4},{6,7},{7,6},{8,9},{9,8},{10,11... | collective-permute-start | bytes 3932168 | tf_op jit(solution)/shard_map/ppermute | solution.py:249
  485.6 46.5 %collective-permute-start.24 = (bf16[10,32,2048]{2,1,0:T(8,128)(2,1)}, bf16[10,32,2048]{2,1,0:T(8,128)(2,1)}, u32[]{:S(2)}, u32[]{:S(2)}) collective-permute-start(bf16[10,32,2048]{2,1,0:T(8,128)(2,1)} %collective-permute-done.22.refs_1_), channel_id=1, source_target_pairs={{0,1},{1,0},{2,3},{3,2},{4,5},{5,4},{6,7},{7,6},{8,9},{9,8},{10,11... | collective-permute-start | bytes 3932168 | tf_op jit(solution)/shard_map/ppermute | solution.py:249
  485.9 56.4 %collective-permute-start.20 = (bf16[10,32,2048]{2,1,0:T(8,128)(2,1)}, bf16[10,32,2048]{2,1,0:T(8,128)(2,1)S(1)}, u32[]{:S(2)}, u32[]{:S(2)}) collective-permute-start(bf16[10,32,2048]{2,1,0:T(8,128)(2,1)} %collective-permute-done.18.refs_0_), channel_id=1, source_target_pairs={{0,1},{1,0},{2,3},{3,2},{4,5},{5,4},{6,7},{7,6},{8,9},{9,8},{10,11... | collective-permute-start | bytes 3932168 | tf_op jit(solution)/shard_map/ppermute | solution.py:249
  521.6 69.3 %collective-permute-start.33 = (bf16[512,2048]{1,0:T(8,128)(2,1)}, bf16[512,2048]{1,0:T(8,128)(2,1)}, u32[]{:S(2)}, u32[]{:S(2)}) collective-permute-start(bf16[512,2048]{1,0:T(8,128)(2,1)} %param.9), channel_id=1, source_target_pairs={{0,1},{1,0},{2,3},{3,2},{4,5},{5,4},{6,7},{7,6},{8,9},{9,8},{10,11... | collective-permute-start | bytes 6291464 | tf_op jit(solution)/shard_map/ppermute | solution.py:249
  532.0 58.9 %collective-permute-start.34 = (bf16[512,2048]{1,0:T(8,128)(2,1)}, bf16[512,2048]{1,0:T(8,128)(2,1)}, u32[]{:S(2)}, u32[]{:S(2)}) collective-permute-start(bf16[512,2048]{1,0:T(8,128)(2,1)} %collective-permute-done.2), channel_id=1, source_target_pairs={{0,1},{1,0},{2,3},{3,2},{4,5},{5,4},{6,7},{7,6},{8,9},{9,8},{10,11... | collective-permute-start | bytes 6291464 | tf_op jit(solution)/shard_map/ppermute | solution.py:249
  (21 other events, 320.9 us)

commit v3 on v2

--- a/solution.py
+++ b/solution.py
@@ -132,6 +132,46 @@
     )(*operands)
 
 
+def project_own_kernel(block, weight, query_weight, mark, out, queries):
+    project_kernel(1, block, weight, out)
+    tiles, height, depth = block.shape
+    queries[...] = jnp.dot(
+        block[...].reshape(tiles * height, depth),
+        query_weight[...],
+        preferred_element_type=jnp.float32,
+    ).astype(queries.dtype)
+
+
+def project_own(normed, weight, query_weight, slots, step, mark):
+    tiles, height, depth = normed.shape
+    width, query_width = weight.shape[1], query_weight.shape[1]
+    rows = tiles * height
+    return pl.pallas_call(
+        project_own_kernel,
+        grid=(tiles // step,),
+        in_specs=[
+            pl.BlockSpec((step, height, depth), lambda i: (i, 0, 0)),
+            pl.BlockSpec((depth, width), lambda i: (0, 0)),
+            pl.BlockSpec((depth, query_width), lambda i: (0, 0)),
+            pl.BlockSpec(memory_space=pl.ANY),
+        ],
+        out_specs=[
+            pl.BlockSpec((step, height, width), lambda i: (i, 0, 0)),
+            pl.BlockSpec((step * height, query_width), lambda i: (i, 0)),
+        ],
+        out_shape=[
+            jax.ShapeDtypeStruct((slots, height, width), jnp.bfloat16),
+            jax.ShapeDtypeStruct((rows, query_width), jnp.bfloat16),
+        ],
+        compiler_params=pltpu.CompilerParams(vmem_limit_bytes=VMEM),
+        cost_estimate=pl.CostEstimate(
+            flops=2 * rows * depth * (width + query_width),
+            bytes_accessed=2 * (rows + depth) * (depth + width + query_width),
+            transcendentals=0,
+        ),
+    )(normed, weight, query_weight, mark)
+
+
 def attend_kernel(tile_ids, slot_ids, query, *refs):
     blocks, out = refs[:KT], refs[KT]
     width = query.shape[1]
@@ -142,8 +182,9 @@
         values = jnp.concatenate([ref[0, :, at_value] for ref in blocks], axis=0)
         scores = lax.dot_general(
             query[:, at], keys, (((1,), (1,)), ((), ())), preferred_element_type=jnp.float32
-        ) * (1.0 / math.sqrt(HD))
-        exponent = jnp.exp(scores - jnp.max(scores, axis=-1, keepdims=True))
+        )
+        maxima = jnp.max(scores, axis=-1, keepdims=True)
+        exponent = jnp.exp2((scores - maxima) * (math.log2(math.e) / math.sqrt(HD)))
         total = jnp.sum(exponent, axis=-1, keepdims=True)
         summed = jnp.dot(
             exponent.astype(jnp.bfloat16), values, preferred_element_type=jnp.float32
@@ -215,10 +256,11 @@
             num_scalar_prefetch=2,
             grid=(1,),
             in_specs=[pl.BlockSpec(memory_space=pl.ANY)] * len(sources),
-            out_specs=[pl.BlockSpec(memory_space=pl.ANY)] * len(lists),
+            out_specs=[pl.BlockSpec(shape.shape, lambda i, which, ids: (0, 0, 0))] * len(lists),
             scratch_shapes=[pltpu.SemaphoreType.DMA((capacity * len(lists),))],
         ),
         out_shape=[shape] * len(lists),
+        compiler_params=pltpu.CompilerParams(vmem_limit_bytes=VMEM),
         cost_estimate=pl.CostEstimate(flops=0, bytes_accessed=4 * size, transcendentals=0),
     )(which.reshape(1), jnp.concatenate(lists), *sources)
 
@@ -242,7 +284,9 @@
         down = lax.ppermute(down, "z", [(i, i - 1) for i in range(1, ZS - s + 1)])
         return up, down
 
-    def across(a):
+    def across(a, *results):
+        if results:
+            a = lax.optimization_barrier((a, results))[0]
         return lax.ppermute(a, "y", SWAP)
 
     def aside(a):
@@ -268,14 +312,9 @@
     w_across = across(out_weight)
 
     normed = normalize(tokens, norm_gain)
-    queries = jnp.dot(
-        normed, in_weight[:, 0, :], preferred_element_type=jnp.float32
-    ).astype(jnp.bfloat16)
+    query_weight = in_weight[:, 0, :]
     weight = in_weight[:, 1:, :].reshape(depth, 2 * head_width)
     slots = OWN_SLOTS + capacity * (2 * ZS - 1)
-    buffer = project(
-        [(normed.reshape(tile_count, TILE, depth), 0)], tile_count, weight, slots, 0, 4, None
-    )
 
     def after(lists, *results):
         return lax.optimization_barrier((lists, results))[0]
@@ -291,11 +330,14 @@
     def quarters(a, b):
         return [(a, 0), (b, 0), (aside(a), 0), (aside(b), 0)]
 
-    lists = after((my_lists, beside_lists), ups[1], downs[1], buffer, queries, w_across)
+    lists = after((my_lists, beside_lists), ups[1], downs[1], normed, weight, w_across)
     ups[2], downs[2] = line(ups[1], downs[1], 2)
     own1, out1 = choose(1, lists, [downs[1], ups[1]], z % 2)
-    rx1, own1y = over(out1), across(own1)
+    rx1, own1y = over(out1), across(own1, rx0, w_across)
     side0 = aside(rx0)
+    buffer, queries = project_own(
+        normed.reshape(tile_count, TILE, depth), weight, query_weight, slots, 4, lists[0]
+    )
     buffer = place(
         0, [(rx0, 0), (rx0, capacity), (side0, 0), (side0, capacity)], buffer
     )
@@ -303,17 +345,20 @@
     lists = after(lists, ups[2], downs[2], rx1, own1y, buffer)
     ups[3], downs[3] = line(ups[2], downs[2], 3)
     own2, out2 = choose(2, lists, [downs[2], downs[1], ups[1], ups[2]], z)
-    rx1y, rx2, own2y = across(rx1), over(out2), across(own2)
+    rx2, rx1y = over(out2), across(rx1, own1y)
+    own2y = across(own2, rx1y)
     buffer = place(1, quarters(own1, own1y), buffer)
     buffer = place(2, quarters(rx1, rx1y), buffer)
 
-    lists = after(lists, ups[3], downs[3], rx2, own2y, buffer)
+    lists = after(lists, ups[3], downs[3], rx2)
     own3, out3 = choose(3, lists, [downs[3], downs[2], ups[2], ups[3]], z)
-    rx2y, rx3, own3y = across(rx2), over(out3), across(own3)
+    rx3, rx2y = over(out3), across(rx2, own2y)
+    own3y = across(own3, rx2y)
     buffer = place(3, quarters(own2, own2y), buffer)
+    rx3y = across(rx3, own3y, buffer)
     buffer = place(4, quarters(rx2, rx2y), buffer)
-    rx3y = across(rx3)
     buffer = place(5, quarters(own3, own3y), buffer)
+    rx3y, _ = lax.optimization_barrier((rx3y, buffer))
     buffer = place(6, quarters(rx3, rx3y), buffer)
     out_all = jnp.concatenate(
         [out_weight, w_across, aside(out_weight), aside(w_across)], axis=0

time: 604 us -> 357 us (0.59)
  Pallas kernels: 349 us -> 122 us
  waiting for transfers between devices: 157 us -> 148 us
  matrix products: 15.1 us -> 7.83 us
    pallas_call x3, Pallas kernels: 244 us -> 13.4 us  [pick(): pl.pallas_call(lambda *refs: pick_kernel(len(sources), *refs), grid_spec=...]
    pallas_call x0 -> x1, Pallas kernels: none -> 17.5 us  [project_own(): pl.pallas_call(project_own_kernel, grid=(tiles // step,), in_specs=[pl.Bl...]
    ppermute x4, waiting for transfers between devices: 59.5 us -> 42.8 us  [over(): return lax.ppermute(a, 'x', SWAP)]
    pallas_call x8 -> x7, Pallas kernels: 80.9 us -> 66.9 us  [project(): pl.pallas_call(lambda *refs: project_kernel(len(pieces), *refs), grid=(ti...]
    dot_general x1 -> x0, matrix products: 7.22 us -> none  [grid_body(): jnp.dot(normed, in_weight[:, 0, :], preferred_element_type=jnp.float32)]
  transfers between devices with their start and end apart: 35 -> 35, of which waited for: 13 -> 14; matrix products, arithmetic and copies ran while one was open for 8% -> 11% of each run, Pallas kernels for 58% -> 34%
where the time goes in v3:
time: 357 us; the launch traced here: 356 us
  waiting for transfers between devices  148 us (41%)
  Pallas kernels  122 us (34%)
  starting transfers between devices  26.6 us (7%)
  local copies, waits for them, and re-layouts  25.4 us (7%)
  other arithmetic  23.7 us (7%)
  matrix products  7.83 us (2%)
    ppermute x8, waiting for transfers between devices, across(): return lax.ppermute(a, 'y', SWAP)  70.6 us
    pallas_call x7, Pallas kernels, project(): pl.pallas_call(lambda *refs: project_kernel(len(pieces), *refs), grid=(ti...  66.9 us
    ppermute x4, waiting for transfers between devices, over(): return lax.ppermute(a, 'x', SWAP)  42.8 us
    pallas_call x2, Pallas kernels, attend(): pl.pallas_call(attend_kernel, grid_spec=pltpu.PrefetchScalarGridSpec(num_...  23.7 us
    ppermute x3, waiting for transfers between devices, line(): down = lax.ppermute(down, 'z', [(i, i - 1) for i in range(1, ZS - s + 1)])  23.5 us
    pallas_call x1, Pallas kernels, project_own(): pl.pallas_call(project_own_kernel, grid=(tiles // step,), in_specs=[pl.Bl...  17.5 us
    convert_element_type x3, other arithmetic, normalize(): (values * lax.rsqrt(mean_square + 1e-05) * norm_gain).astype(jnp.bfloat16)  14.3 us
    pallas_call x3, Pallas kernels, pick(): pl.pallas_call(lambda *refs: pick_kernel(len(sources), *refs), grid_spec=...  13.4 us
  transfers between devices with their start and end apart: 35, of which 14 were waited for; matrix products, arithmetic and copies ran while one was open for 11% of the time, Pallas kernels for 34%

profile of v3, /device:TPU:0, one launch (start us, length us, event | category | flops | bytes accessed | tf_op | source)
XLA Modules:
  0.0 355.9 jit_solution(2290090952714378165)
XLA Ops:
  5.6 6.2 %collective-permute-start = (bf16[16,32,2048]{2,1,0:T(8,128)(2,1)}, bf16[16,32,2048]{2,1,0:T(8,128)(2,1)}, u32[]{:S(2)}, u32[]{:S(2)}) collective-permute-start(bf16[16,32,2048]{2,1,0:T(8,128)(2,1)} %fusion.16), channel_id=1, source_target_pairs={{0,8},{8,16},{16,24},{1,9},{9,17},{17,25},{2,10},{10,18},{18,26},{... | collective-permute-start | bytes 6291464 | tf_op jit(solution)/shard_map/ppermute | solution.py:283
  41.3 8.7 %fusion.2 = bf16[2048,2048]{1,0:T(8,128)(2,1)} fusion(bf16[2048,2048]{1,0:T(8,128)(2,1)} %param.6, f32[2048]{0:T(1024)S(1)} %copy-done.8, f32[2048]{0:T(1024)S(1)} %add_rsqrt_fusion.2), kind=kLoop, calls=%fused_computation.5 | loop fusion | flops 16777216 | bytes 16793600 | tf_op jit(solution)/shard_map/convert_element_type | solution.py:25
  49.9 5.7 %collective-permute-done.refs_3_.refs_4_ = bf16[16,32,2048]{2,1,0:T(8,128)(2,1)} collective-permute-done((bf16[16,32,2048]{2,1,0:T(8,128)(2,1)}, bf16[16,32,2048]{2,1,0:T(8,128)(2,1)}, u32[]{:S(2)}, u32[]{:S(2)}) %collective-permute-start) | collective-permute-done | bytes 2097184 | tf_op jit(solution)/shard_map/ppermute | solution.py:283
  55.7 5.4 %collective-permute-done.1.refs_2_.refs_3_ = bf16[16,32,2048]{2,1,0:T(8,128)(2,1)} collective-permute-done((bf16[16,32,2048]{2,1,0:T(8,128)(2,1)}, bf16[16,32,2048]{2,1,0:T(8,128)(2,1)}, u32[]{:S(2)}, u32[]{:S(2)}) %collective-permute-start.1) | collective-permute-done | bytes 2097184 | tf_op jit(solution)/shard_map/ppermute | solution.py:284
  61.5 19.7 %collective-permute-done.6.refs_0_.refs_1_ = bf16[20,32,2048]{2,1,0:T(8,128)(2,1)S(1)} collective-permute-done((bf16[20,32,2048]{2,1,0:T(8,128)(2,1)}, bf16[20,32,2048]{2,1,0:T(8,128)(2,1)S(1)}, u32[]{:S(2)}, u32[]{:S(2)}) %collective-permute-start.6) | collective-permute-done | bytes 2621472 | tf_op jit(solution)/shard_map/ppermute | solution.py:296
  94.8 22.0 %collective-permute-done.5.refs_0_ = bf16[10,32,2048]{2,1,0:T(8,128)(2,1)} collective-permute-done((bf16[10,32,2048]{2,1,0:T(8,128)(2,1)}, bf16[10,32,2048]{2,1,0:T(8,128)(2,1)}, u32[]{:S(2)}, u32[]{:S(2)}) %collective-permute-start.5) | collective-permute-done | bytes 1310752 | tf_op jit(solution)/shard_map/ppermute | solution.py:296
  120.4 17.5 %shard_map.64 = (bf16[90,128,1024]{2,1,0:T(8,128)(2,1)}, bf16[2048,512]{1,0:T(8,128)(2,1)S(1)}) custom-call(bf16[16,128,2048]{2,1,0:T(8,128)(2,1)} %bitcast.36, bf16[2048,1024]{1,0:T(8,128)(2,1)} %bitcast.25, bf16[2048,512]{1,0:T(8,128)(2,1)S(1)} %copy-done.2, s32[8,10]{1,0:T(8,128)S(1)} %copy.42.mark), custom_call_target="tpu_custom_call" | custom-call | flops 12884901888 | bytes 29360128 | tf_op jit(solution)/shard_map/pallas_call | solution.py:149
  139.2 9.4 %shard_map.66.refs_5_ = bf16[90,128,1024]{2,1,0:T(8,128)(2,1)} custom-call(bf16[20,32,2048]{2,1,0:T(8,128)(2,1)S(1)} %collective-permute-done.6.refs_0_.refs_1_, bf16[20,32,2048]{2,1,0:T(8,128)(2,1)S(1)} %collective-permute-done.6.refs_0_.refs_1_, bf16[20,32,2048]{2,1,0:T(8,128)(2,1)} %collective-permute-done.8.refs_2_.refs_3_, ...), custom_call_target="tpu_custom_call", output_to_operand_aliasing={{}: (5, {})} | custom-call | flops 5368709120 | bytes 12058624 | tf_op jit(solution)/shard_map/pallas_call | solution.py:119
  156.8 26.4 %collective-permute-done.14.refs_1_ = bf16[10,32,2048]{2,1,0:T(8,128)(2,1)S(1)} collective-permute-done((bf16[10,32,2048]{2,1,0:T(8,128)(2,1)}, bf16[10,32,2048]{2,1,0:T(8,128)(2,1)S(1)}, u32[]{:S(2)}, u32[]{:S(2)}) %collective-permute-start.14) | collective-permute-done | bytes 1310752 | tf_op jit(solution)/shard_map/ppermute | solution.py:290
  185.3 18.1 %collective-permute-done.10.refs_2_ = bf16[16,32,2048]{2,1,0:T(8,128)(2,1)S(1)} collective-permute-done((bf16[16,32,2048]{2,1,0:T(8,128)(2,1)}, bf16[16,32,2048]{2,1,0:T(8,128)(2,1)S(1)}, u32[]{:S(2)}, u32[]{:S(2)}) %collective-permute-start.10) | collective-permute-done | bytes 2097184 | tf_op jit(solution)/shard_map/ppermute | solution.py:284
  203.9 9.0 %collective-permute-done.15.refs_1_ = bf16[10,32,2048]{2,1,0:T(8,128)(2,1)S(1)} collective-permute-done((bf16[10,32,2048]{2,1,0:T(8,128)(2,1)S(1)}, bf16[10,32,2048]{2,1,0:T(8,128)(2,1)S(1)}, u32[]{:S(2)}, u32[]{:S(2)}) %collective-permute-start.15) | collective-permute-done | bytes 1310752 | tf_op jit(solution)/shard_map/ppermute | solution.py:290
  215.1 5.5 %shard_map.68 = (bf16[10,32,2048]{2,1,0:T(8,128)(2,1)S(1)}, bf16[10,32,2048]{2,1,0:T(8,128)(2,1)}) custom-call(s32[1]{0:T(128)} %bitcast.6.refs_0_, s32[20]{0:T(128)S(1)} %pad_add_fusion.3.refs_1_, bf16[16,32,2048]{2,1,0:T(8,128)(2,1)S(1)} %collective-permute-done.10.refs_2_, bf16[16,32,2048]{2,1,0:T(8,128)(2,1)} %collective-permute-done.4.refs_2_.refs_3_, ...), custom_call_target="tpu_custom_call" | custom-call | bytes 5242880 | tf_op jit(solution)/shard_map/pallas_call | solution.py:253
  222.0 10.0 %shard_map.69.refs_5_ = bf16[90,128,1024]{2,1,0:T(8,128)(2,1)} custom-call(bf16[10,32,2048]{2,1,0:T(8,128)(2,1)} %get-tuple-element.31.refs_0_, bf16[10,32,2048]{2,1,0:T(8,128)(2,1)} %collective-permute-done.7.refs_1_, bf16[10,32,2048]{2,1,0:T(8,128)(2,1)} %collective-permute-done.21.refs_2_, ...), custom_call_target="tpu_custom_call", output_to_operand_aliasing={{}: (5, {})} | custom-call | flops 5368709120 | bytes 12058624 | tf_op jit(solution)/shard_map/pallas_call | solution.py:119
  232.5 10.1 %shard_map.70.refs_5_ = bf16[90,128,1024]{2,1,0:T(8,128)(2,1)} custom-call(bf16[10,32,2048]{2,1,0:T(8,128)(2,1)} %collective-permute-done.5.refs_0_, bf16[10,32,2048]{2,1,0:T(8,128)(2,1)} %collective-permute-done.13.refs_1_, bf16[10,32,2048]{2,1,0:T(8,128)(2,1)} %collective-permute-done.19.refs_2_, ...), custom_call_target="tpu_custom_call", output_to_operand_aliasing={{}: (5, {})} | custom-call | flops 5368709120 | bytes 12058624 | tf_op jit(solution)/shard_map/pallas_call | solution.py:119
  242.7 9.1 %collective-permute-done.16.refs_1_ = bf16[10,32,2048]{2,1,0:T(8,128)(2,1)S(1)} collective-permute-done((bf16[10,32,2048]{2,1,0:T(8,128)(2,1)S(1)}, bf16[10,32,2048]{2,1,0:T(8,128)(2,1)S(1)}, u32[]{:S(2)}, u32[]{:S(2)}) %collective-permute-start.16) | collective-permute-done | bytes 1310752 | tf_op jit(solution)/shard_map/ppermute | solution.py:290
  251.8 9.4 %shard_map.71.refs_5_ = bf16[90,128,1024]{2,1,0:T(8,128)(2,1)} custom-call(bf16[10,32,2048]{2,1,0:T(8,128)(2,1)} %get-tuple-element.42.refs_0_, bf16[10,32,2048]{2,1,0:T(8,128)(2,1)S(1)} %copy-done.4, bf16[10,32,2048]{2,1,0:T(8,128)(2,1)} %collective-permute-done.17.refs_2_, ...), custom_call_target="tpu_custom_call", output_to_operand_aliasing={{}: (5, {})} | custom-call | flops 5368709120 | bytes 12058624 | tf_op jit(solution)/shard_map/pallas_call | solution.py:119
  262.3 9.0 %shard_map.72.refs_5_ = bf16[90,128,1024]{2,1,0:T(8,128)(2,1)} custom-call(bf16[10,32,2048]{2,1,0:T(8,128)(2,1)S(1)} %collective-permute-done.11.refs_0_, bf16[10,32,2048]{2,1,0:T(8,128)(2,1)S(1)} %copy-done.6, bf16[10,32,2048]{2,1,0:T(8,128)(2,1)S(1)} %collective-permute-done.26.refs_2_, ...), custom_call_target="tpu_custom_call", output_to_operand_aliasing={{}: (5, {})} | custom-call | flops 5368709120 | bytes 12058624 | tf_op jit(solution)/shard_map/pallas_call | solution.py:119
  271.3 9.0 %shard_map.73.refs_5_ = bf16[90,128,1024]{2,1,0:T(8,128)(2,1)} custom-call(bf16[10,32,2048]{2,1,0:T(8,128)(2,1)S(1)} %get-tuple-element.44.refs_0_, bf16[10,32,2048]{2,1,0:T(8,128)(2,1)S(1)} %collective-permute-done.16.refs_1_, bf16[10,32,2048]{2,1,0:T(8,128)(2,1)S(1)} %collective-permute-done.24.refs_2_, ...), custom_call_target="tpu_custom_call", output_to_operand_aliasing={{}: (5, {})} | custom-call | flops 5368709120 | bytes 12058624 | tf_op jit(solution)/shard_map/pallas_call | solution.py:119
  280.3 12.4 %collective-permute-done.23.refs_1_ = bf16[10,32,2048]{2,1,0:T(8,128)(2,1)} collective-permute-done((bf16[10,32,2048]{2,1,0:T(8,128)(2,1)}, bf16[10,32,2048]{2,1,0:T(8,128)(2,1)}, u32[]{:S(2)}, u32[]{:S(2)}) %collective-permute-start.23) | collective-permute-done | bytes 1310752 | tf_op jit(solution)/shard_map/ppermute | solution.py:290
  297.8 9.8 %shard_map.74.refs_0_.refs_1_.refs_2_.refs_3_ = bf16[90,128,1024]{2,1,0:T(8,128)(2,1)} custom-call(bf16[10,32,2048]{2,1,0:T(8,128)(2,1)} %collective-permute-done.12.refs_0_, bf16[10,32,2048]{2,1,0:T(8,128)(2,1)} %collective-permute-done.23.refs_1_, bf16[10,32,2048]{2,1,0:T(8,128)(2,1)} %collective-permute-done.28.refs_2_, ...), custom_call_target="tpu_custom_call", output_to_operand_aliasing={{}: (5, {})} | custom-call | flops 5368709120 | bytes 12058624 | tf_op jit(solution)/shard_map/pallas_call | solution.py:119
  307.7 11.7 %shard_map.76 = bf16[1024,512]{1,0:T(8,128)(2,1)S(1)} custom-call(s32[8]{0:T(128)S(1)} %iota_add_fusion.tile_ids, s32[32]{0:T(128)S(1)} %reshape.322.slot_ids, bf16[2048,512]{1,0:T(8,128)(2,1)S(1)} %copy-done.1, bf16[90,128,1024]{2,1,0:T(8,128)(2,1)} %shard_map.74.refs_0_.refs_1_.refs_2_.refs_3_, ...), custom_call_target="tpu_custom_call" | custom-call | flops 1073741824 | bytes 10485760 | tf_op jit(solution)/shard_map/pallas_call | solution.py:201
  320.4 12.0 %shard_map.75 = bf16[1024,512]{1,0:T(8,128)(2,1)S(1)} custom-call(s32[8]{0:T(128)S(1)} %iota_add_fusion.1.tile_ids, s32[32]{0:T(128)S(1)} %reshape.314.slot_ids, bf16[2048,512]{1,0:T(8,128)(2,1)S(1)} %copy-done.1, bf16[90,128,1024]{2,1,0:T(8,128)(2,1)} %shard_map.74.refs_0_.refs_1_.refs_2_.refs_3_, ...), custom_call_target="tpu_custom_call" | custom-call | flops 1073741824 | bytes 10485760 | tf_op jit(solution)/shard_map/pallas_call | solution.py:201
  332.6 12.2 %collective-permute-done.30 = bf16[1024,512]{1,0:T(8,128)(2,1)} collective-permute-done((bf16[1024,512]{1,0:T(8,128)(2,1)S(1)}, bf16[1024,512]{1,0:T(8,128)(2,1)}, u32[]{:S(2)}, u32[]{:S(2)}) %collective-permute-start.30) | collective-permute-done | bytes 1048608 | tf_op jit(solution)/shard_map/ppermute | solution.py:290
  348.0 7.8 %fusion.17 = bf16[512,2048]{1,0:T(8,128)(2,1)} fusion(bf16[512,2048]{1,0:T(8,128)(2,1)} %collective-permute-done.34, bf16[512,2048]{1,0:T(8,128)(2,1)} %collective-permute-done.33, bf16[512,2048]{1,0:T(8,128)(2,1)} %collective-permute-done.2, bf16[512,2048]{1,0:T(8,128)(2,1)} %param.9, bf16[512,512]{1,0:T(8,128)(2,1)S(1)} %collective-permute-done.32, ...), kind=kOutput, calls=%fused_computation.25 | convolution fusion | flops 4337958912 | bytes 12582912 | tf_op jit(solution)/shard_map/dot_general | solution.py:396
  (139 shorter events, 77.1 us)
Async XLA Ops:
  5.6 50.1 %collective-permute-start = (bf16[16,32,2048]{2,1,0:T(8,128)(2,1)}, bf16[16,32,2048]{2,1,0:T(8,128)(2,1)}, u32[]{:S(2)}, u32[]{:S(2)}) collective-permute-start(bf16[16,32,2048]{2,1,0:T(8,128)(2,1)} %fusion.16), channel_id=1, source_target_pairs={{0,8},{8,16},{16,24},{1,9},{9,17},{17,25},{2,10},{10,18},{18,26},{... | collective-permute-start | bytes 6291464 | tf_op jit(solution)/shard_map/ppermute | solution.py:283
  11.8 49.3 %collective-permute-start.1 = (bf16[16,32,2048]{2,1,0:T(8,128)(2,1)}, bf16[16,32,2048]{2,1,0:T(8,128)(2,1)}, u32[]{:S(2)}, u32[]{:S(2)}) collective-permute-start(bf16[16,32,2048]{2,1,0:T(8,128)(2,1)} %fusion.16), channel_id=1, source_target_pairs={{8,0},{16,8},{24,16},{9,1},{17,9},{25,17},{10,2},{18,10},{26,18},{... | collective-permute-start | bytes 6291464 | tf_op jit(solution)/shard_map/ppermute | solution.py:284
  13.1 48.0 %collective-permute-start.2 = (bf16[512,2048]{1,0:T(8,128)(2,1)}, bf16[512,2048]{1,0:T(8,128)(2,1)}, u32[]{:S(2)}, u32[]{:S(2)}) collective-permute-start(bf16[512,2048]{1,0:T(8,128)(2,1)} %param.9), channel_id=1, source_target_pairs={{0,2},{2,0},{1,3},{3,1},{4,6},{6,4},{5,7},{7,5},{8,10},{10,8},{9,1... | collective-permute-start | bytes 6291464 | tf_op jit(solution)/shard_map/ppermute | solution.py:290
  22.9 58.3 %collective-permute-start.6 = (bf16[20,32,2048]{2,1,0:T(8,128)(2,1)}, bf16[20,32,2048]{2,1,0:T(8,128)(2,1)S(1)}, u32[]{:S(2)}, u32[]{:S(2)}) collective-permute-start(bf16[20,32,2048]{2,1,0:T(8,128)(2,1)} %fusion.13), channel_id=1, source_target_pairs={{0,4},{4,0},{1,5},{5,1},{2,6},{6,2},{3,7},{7,3},{8,12},{12,8},{9,1... | collective-permute-start | bytes 7864328 | tf_op jit(solution)/shard_map/ppermute | solution.py:296
  81.2 58.1 %collective-permute-start.8 = (bf16[20,32,2048]{2,1,0:T(8,128)(2,1)S(1)}, bf16[20,32,2048]{2,1,0:T(8,128)(2,1)}, u32[]{:S(2)}, u32[]{:S(2)}) collective-permute-start(bf16[20,32,2048]{2,1,0:T(8,128)(2,1)S(1)} %collective-permute-done.6.refs_0_.refs_1_), channel_id=1, source_target_pairs={{0,1},{1,0},{2,3},{3,2},{4,5},{5,4},{6,7},{7,6},{8,9},{9,8},{10,11... | collective-permute-start | bytes 7864328 | tf_op jit(solution)/shard_map/ppermute | solution.py:293
  85.2 31.6 %collective-permute-start.5 = (bf16[10,32,2048]{2,1,0:T(8,128)(2,1)}, bf16[10,32,2048]{2,1,0:T(8,128)(2,1)}, u32[]{:S(2)}, u32[]{:S(2)}) collective-permute-start(bf16[10,32,2048]{2,1,0:T(8,128)(2,1)} %get-tuple-element.29), channel_id=1, source_target_pairs={{0,4},{4,0},{1,5},{5,1},{2,6},{6,2},{3,7},{7,3},{8,12},{12,8},{9,1... | collective-permute-start | bytes 3932168 | tf_op jit(solution)/shard_map/ppermute | solution.py:296
  87.1 31.2 %collective-permute-start.7 = (bf16[10,32,2048]{2,1,0:T(8,128)(2,1)}, bf16[10,32,2048]{2,1,0:T(8,128)(2,1)}, u32[]{:S(2)}, u32[]{:S(2)}) collective-permute-start(bf16[10,32,2048]{2,1,0:T(8,128)(2,1)} %get-tuple-element.31.refs_0_), channel_id=1, source_target_pairs={{0,2},{2,0},{1,3},{3,1},{4,6},{6,4},{5,7},{7,5},{8,10},{10,8},{9,1... | collective-permute-start | bytes 3932168 | tf_op jit(solution)/shard_map/ppermute | solution.py:290
  88.2 60.5 %collective-permute-start.3 = (bf16[16,32,2048]{2,1,0:T(8,128)(2,1)}, bf16[16,32,2048]{2,1,0:T(8,128)(2,1)}, u32[]{:S(2)}, u32[]{:S(2)}) collective-permute-start(bf16[16,32,2048]{2,1,0:T(8,128)(2,1)} %collective-permute-done.refs_3_.refs_4_), channel_id=1, source_target_pairs={{8,16},{16,24},{9,17},{17,25},{10,18},{18,26},{11,19},{19,27},{12,... | collective-permute-start | bytes 6291464 | tf_op jit(solution)/shard_map/ppermute | solution.py:283
  90.2 58.5 %collective-permute-start.4 = (bf16[16,32,2048]{2,1,0:T(8,128)(2,1)}, bf16[16,32,2048]{2,1,0:T(8,128)(2,1)}, u32[]{:S(2)}, u32[]{:S(2)}) collective-permute-start(bf16[16,32,2048]{2,1,0:T(8,128)(2,1)} %collective-permute-done.1.refs_2_.refs_3_), channel_id=1, source_target_pairs={{8,0},{16,8},{9,1},{17,9},{10,2},{18,10},{11,3},{19,11},{12,4},{20... | collective-permute-start | bytes 6291464 | tf_op jit(solution)/shard_map/ppermute | solution.py:284
  118.3 34.8 %collective-permute-start.13 = (bf16[10,32,2048]{2,1,0:T(8,128)(2,1)}, bf16[10,32,2048]{2,1,0:T(8,128)(2,1)}, u32[]{:S(2)}, u32[]{:S(2)}) collective-permute-start(bf16[10,32,2048]{2,1,0:T(8,128)(2,1)} %collective-permute-done.5.refs_0_), channel_id=1, source_target_pairs={{0,2},{2,0},{1,3},{3,1},{4,6},{6,4},{5,7},{7,5},{8,10},{10,8},{9,1... | collective-permute-start | bytes 3932168 | tf_op jit(solution)/shard_map/ppermute | solution.py:290
  153.1 30.1 %collective-permute-start.14 = (bf16[10,32,2048]{2,1,0:T(8,128)(2,1)}, bf16[10,32,2048]{2,1,0:T(8,128)(2,1)S(1)}, u32[]{:S(2)}, u32[]{:S(2)}) collective-permute-start(bf16[10,32,2048]{2,1,0:T(8,128)(2,1)} %get-tuple-element.42.refs_0_), channel_id=1, source_target_pairs={{0,2},{2,0},{1,3},{3,1},{4,6},{6,4},{5,7},{7,5},{8,10},{10,8},{9,1... | collective-permute-start | bytes 3932168 | tf_op jit(solution)/shard_map/ppermute | solution.py:290
  154.7 29.5 %collective-permute-start.11 = (bf16[10,32,2048]{2,1,0:T(8,128)(2,1)S(1)}, bf16[10,32,2048]{2,1,0:T(8,128)(2,1)S(1)}, u32[]{:S(2)}, u32[]{:S(2)}) collective-permute-start(bf16[10,32,2048]{2,1,0:T(8,128)(2,1)S(1)} %get-tuple-element.35), channel_id=1, source_target_pairs={{0,4},{4,0},{1,5},{5,1},{2,6},{6,2},{3,7},{7,3},{8,12},{12,8},{9,1... | collective-permute-start | bytes 3932168 | tf_op jit(solution)/shard_map/ppermute | solution.py:296
  154.7 48.6 %collective-permute-start.10 = (bf16[16,32,2048]{2,1,0:T(8,128)(2,1)}, bf16[16,32,2048]{2,1,0:T(8,128)(2,1)S(1)}, u32[]{:S(2)}, u32[]{:S(2)}) collective-permute-start(bf16[16,32,2048]{2,1,0:T(8,128)(2,1)} %collective-permute-done.4.refs_2_.refs_3_), channel_id=1, source_target_pairs={{8,0},{9,1},{10,2},{11,3},{12,4},{13,5},{14,6},{15,7}} | collective-permute-start | bytes 6291464 | tf_op jit(solution)/shard_map/ppermute | solution.py:284
  156.0 47.4 %collective-permute-start.9 = (bf16[16,32,2048]{2,1,0:T(8,128)(2,1)}, bf16[16,32,2048]{2,1,0:T(8,128)(2,1)S(1)}, u32[]{:S(2)}, u32[]{:S(2)}) collective-permute-start(bf16[16,32,2048]{2,1,0:T(8,128)(2,1)} %collective-permute-done.3.refs_5_.refs_4_), channel_id=1, source_target_pairs={{16,24},{17,25},{18,26},{19,27},{20,28},{21,29},{22,30},{23,31}} | collective-permute-start | bytes 6291464 | tf_op jit(solution)/shard_map/ppermute | solution.py:283
  184.8 35.8 %collective-permute-start.21 = (bf16[10,32,2048]{2,1,0:T(8,128)(2,1)}, bf16[10,32,2048]{2,1,0:T(8,128)(2,1)}, u32[]{:S(2)}, u32[]{:S(2)}) collective-permute-start(bf16[10,32,2048]{2,1,0:T(8,128)(2,1)} %get-tuple-element.31.refs_0_), channel_id=1, source_target_pairs={{0,1},{1,0},{2,3},{3,2},{4,5},{5,4},{6,7},{7,6},{8,9},{9,8},{10,11... | collective-permute-start | bytes 3932168 | tf_op jit(solution)/shard_map/ppermute | solution.py:293
  184.8 35.9 %collective-permute-start.19 = (bf16[10,32,2048]{2,1,0:T(8,128)(2,1)}, bf16[10,32,2048]{2,1,0:T(8,128)(2,1)}, u32[]{:S(2)}, u32[]{:S(2)}) collective-permute-start(bf16[10,32,2048]{2,1,0:T(8,128)(2,1)} %collective-permute-done.5.refs_0_), channel_id=1, source_target_pairs={{0,1},{1,0},{2,3},{3,2},{4,5},{5,4},{6,7},{7,6},{8,9},{9,8},{10,11... | collective-permute-start | bytes 3932168 | tf_op jit(solution)/shard_map/ppermute | solution.py:293
  220.6 31.2 %collective-permute-start.16 = (bf16[10,32,2048]{2,1,0:T(8,128)(2,1)S(1)}, bf16[10,32,2048]{2,1,0:T(8,128)(2,1)S(1)}, u32[]{:S(2)}, u32[]{:S(2)}) collective-permute-start(bf16[10,32,2048]{2,1,0:T(8,128)(2,1)S(1)} %get-tuple-element.44.refs_0_), channel_id=1, source_target_pairs={{0,2},{2,0},{1,3},{3,1},{4,6},{6,4},{5,7},{7,5},{8,10},{10,8},{9,1... | collective-permute-start | bytes 3932168 | tf_op jit(solution)/shard_map/ppermute | solution.py:290
  221.5 39.8 %collective-permute-start.12 = (bf16[10,32,2048]{2,1,0:T(8,128)(2,1)}, bf16[10,32,2048]{2,1,0:T(8,128)(2,1)}, u32[]{:S(2)}, u32[]{:S(2)}) collective-permute-start(bf16[10,32,2048]{2,1,0:T(8,128)(2,1)} %get-tuple-element.38), channel_id=1, source_target_pairs={{0,4},{4,0},{1,5},{5,1},{2,6},{6,2},{3,7},{7,3},{8,12},{12,8},{9,1... | collective-permute-start | bytes 3932168 | tf_op jit(solution)/shard_map/ppermute | solution.py:296
  232.0 30.0 %collective-permute-start.26 = (bf16[10,32,2048]{2,1,0:T(8,128)(2,1)S(1)}, bf16[10,32,2048]{2,1,0:T(8,128)(2,1)S(1)}, u32[]{:S(2)}, u32[]{:S(2)}) collective-permute-start(bf16[10,32,2048]{2,1,0:T(8,128)(2,1)S(1)} %collective-permute-done.11.refs_0_), channel_id=1, source_target_pairs={{0,1},{1,0},{2,3},{3,2},{4,5},{5,4},{6,7},{7,6},{8,9},{9,8},{10,11... | collective-permute-start | bytes 3932168 | tf_op jit(solution)/shard_map/ppermute | solution.py:293
  232.0 30.2 %collective-permute-start.27 = (bf16[10,32,2048]{2,1,0:T(8,128)(2,1)S(1)}, bf16[10,32,2048]{2,1,0:T(8,128)(2,1)S(1)}, u32[]{:S(2)}, u32[]{:S(2)}) collective-permute-start(bf16[10,32,2048]{2,1,0:T(8,128)(2,1)S(1)} %copy-done.6), channel_id=1, source_target_pairs={{0,1},{1,0},{2,3},{3,2},{4,5},{5,4},{6,7},{7,6},{8,9},{9,8},{10,11... | collective-permute-start | bytes 3932168 | tf_op jit(solution)/shard_map/ppermute | solution.py:293
  261.3 31.5 %collective-permute-start.23 = (bf16[10,32,2048]{2,1,0:T(8,128)(2,1)}, bf16[10,32,2048]{2,1,0:T(8,128)(2,1)}, u32[]{:S(2)}, u32[]{:S(2)}) collective-permute-start(bf16[10,32,2048]{2,1,0:T(8,128)(2,1)} %collective-permute-done.12.refs_0_), channel_id=1, source_target_pairs={{0,2},{2,0},{1,3},{3,1},{4,6},{6,4},{5,7},{7,5},{8,10},{10,8},{9,1... | collective-permute-start | bytes 3932168 | tf_op jit(solution)/shard_map/ppermute | solution.py:290
  262.0 31.9 %collective-permute-start.28 = (bf16[10,32,2048]{2,1,0:T(8,128)(2,1)}, bf16[10,32,2048]{2,1,0:T(8,128)(2,1)}, u32[]{:S(2)}, u32[]{:S(2)}) collective-permute-start(bf16[10,32,2048]{2,1,0:T(8,128)(2,1)} %collective-permute-done.12.refs_0_), channel_id=1, source_target_pairs={{0,1},{1,0},{2,3},{3,2},{4,5},{5,4},{6,7},{7,6},{8,9},{9,8},{10,11... | collective-permute-start | bytes 3932168 | tf_op jit(solution)/shard_map/ppermute | solution.py:293
  292.8 53.4 %collective-permute-start.33 = (bf16[512,2048]{1,0:T(8,128)(2,1)}, bf16[512,2048]{1,0:T(8,128)(2,1)}, u32[]{:S(2)}, u32[]{:S(2)}) collective-permute-start(bf16[512,2048]{1,0:T(8,128)(2,1)} %param.9), channel_id=1, source_target_pairs={{0,1},{1,0},{2,3},{3,2},{4,5},{5,4},{6,7},{7,6},{8,9},{9,8},{10,11... | collective-permute-start | bytes 6291464 | tf_op jit(solution)/shard_map/ppermute | solution.py:293
  293.8 52.3 %collective-permute-start.34 = (bf16[512,2048]{1,0:T(8,128)(2,1)}, bf16[512,2048]{1,0:T(8,128)(2,1)}, u32[]{:S(2)}, u32[]{:S(2)}) collective-permute-start(bf16[512,2048]{1,0:T(8,128)(2,1)} %collective-permute-done.2), channel_id=1, source_target_pairs={{0,1},{1,0},{2,3},{3,2},{4,5},{5,4},{6,7},{7,6},{8,9},{9,8},{10,11... | collective-permute-start | bytes 6291464 | tf_op jit(solution)/shard_map/ppermute | solution.py:293
  (21 other events, 298.1 us)
